TPU v7x, 1024 devices: a whole 8x8x8 slice. The times are simulated.
1024 devices in a mesh: group: 16 (over z, core), local: 64 (over y, x).
Axes of the slice: x: 8, y: 8, z: 8, core: 2. Of those that a mesh axis runs over, the one named last changes fastest.
Arguments:
- tokens: bfloat16 [2048, 4096], P(('group', 'local')), may hold values from -6 to 6
- cotangent: bfloat16 [2048, 4096], P(('group', 'local')), may hold values from -6 to 6
- gates: bfloat16 [2048, 8], P(('group', 'local')), may hold values from 0.049804688 to 1
- expert_ids: int32 [2048, 8], P(('group', 'local')), may hold values from 0 to 127, as said below
- capacity: int32 [128], replicated, may hold values from 5 to 10, as said below
- w_gate: bfloat16 [524288, 1024], P(('group', 'local')), may hold values from -0.09375 to 0.09375
- w_up: bfloat16 [524288, 1024], P(('group', 'local')), may hold values from -0.09375 to 0.09375
- w_down: bfloat16 [1024, 524288], P(None, ('group', 'local')), may hold values from -0.1875 to 0.1875
Outputs:
- mixed: bfloat16 [2048, 4096], P(('group', 'local'))
- token_grad: bfloat16 [2048, 4096], P(('group', 'local'))
Inputs may be any that keep to these rules, and one draw needn't show every extreme that they name: `expert_ids`: each row names 8 different experts, all of them in at most 4 groups, expert e lying in group e // 8. capacity[e] is the most rows that expert e takes from the tokens of one group.
All inputs are finite; a program needn't handle non-finite values.
Results may differ from a plain program's by a relative error of at most 0.007.
Values may be sent and summed in bfloat16 or wider, within the bound.
A program may use at most 32 MiB of HBM per device.

v0:
```python
import jax
import jax.numpy as jnp
from jax import lax
from jax.sharding import PartitionSpec as P

SLICES = 8


def from_partner(block, axis, distance):
    count = lax.axis_size(axis)
    route = []
    for low in range(count):
        high = low | 1 << distance
        if high != low and high < count:
            route += [(low, high), (high, low)]
    return lax.ppermute(block, axis, route)


def pair_swap(values, bit_index):
    return from_partner(values, "local", bit_index)


def cross_groups(values):
    return lax.all_to_all(values, "group", split_axis=0, concat_axis=0, tiled=True)


def whole_sum(values, bit_count):
    for bit_index in range(bit_count):
        values = values + pair_swap(values, bit_index)
    return values


def activate(gate_pre, up_pre):
    return (gate_pre * jax.nn.sigmoid(gate_pre) * up_pre).astype(jnp.bfloat16)


def gate_grads(gate_pre, up_pre, d_hidden):
    sigmoid_gate = jax.nn.sigmoid(gate_pre)
    activated = gate_pre * sigmoid_gate
    d_gate = (d_hidden * up_pre * sigmoid_gate * (1.0 + gate_pre * (1.0 - sigmoid_gate))).astype(
        jnp.bfloat16
    )
    d_up = (d_hidden * activated).astype(jnp.bfloat16)
    return (d_gate, d_up)


def per_device(tokens, cotangent, gates, expert_ids, capacity, w_gate, w_up, w_down):
    local_count = lax.axis_size("local")
    group_count = lax.axis_size("group")
    local_index = lax.axis_index("local")
    token_count = tokens.shape[0]
    top_count = expert_ids.shape[1]
    slice_width = w_gate.shape[0]
    hidden_units = w_gate.shape[1]
    expert_total = capacity.shape[0]
    per_group = local_count // SLICES
    bit_count = SLICES.bit_length() - 1
    expert_local = local_index // SLICES
    group_tokens = token_count * local_count
    slot_count = min(group_tokens * top_count // expert_total * 5 // 4, group_tokens)
    row_total = group_count * slot_count
    paired = jnp.stack([tokens, cotangent], 1).reshape(token_count, 2, SLICES, slice_width)
    paired = jnp.transpose(paired, (2, 0, 1, 3))
    send_rows = jnp.broadcast_to(
        paired[None], (per_group, SLICES, token_count, 2, slice_width)
    ).reshape(group_tokens, 2, slice_width)
    send_gates = jnp.broadcast_to(gates[None], (local_count, token_count, top_count)).reshape(
        group_tokens, top_count
    )
    send_ids = jnp.broadcast_to(expert_ids[None], (local_count, token_count, top_count)).reshape(
        group_tokens, top_count
    )
    row_block, gate_block, id_block = (
        lax.all_to_all(send_rows, "local", split_axis=0, concat_axis=0, tiled=True),
        lax.all_to_all(send_gates, "local", split_axis=0, concat_axis=0, tiled=True),
        lax.all_to_all(send_ids, "local", split_axis=0, concat_axis=0, tiled=True),
    )
    targets = jnp.arange(group_count, dtype=jnp.int32) * per_group + expert_local
    matches = id_block[:, None, :] == targets[None, :, None]
    chosen = jnp.any(matches, axis=-1).astype(jnp.int32)
    weight_pair = jnp.sum(
        jnp.where(matches, gate_block[:, None, :], jnp.zeros((), jnp.bfloat16)), axis=-1
    )
    rank_pair = jnp.cumsum(chosen, axis=0) - chosen
    limits = jnp.sum(
        jnp.where(
            jnp.arange(expert_total, dtype=jnp.int32)[None, :] == targets[:, None],
            capacity[None, :],
            0,
        ),
        axis=1,
    )
    kept = (chosen > 0) & (rank_pair < limits[None, :])
    slot_ids = jnp.arange(slot_count, dtype=jnp.int32)
    placed = kept[:, :, None] & (rank_pair[:, :, None] == slot_ids[None, None, :])
    select = placed.astype(jnp.bfloat16)
    outgoing = jnp.einsum(
        "tgc,tkd->gckd", select, row_block, preferred_element_type=jnp.float32
    ).astype(jnp.bfloat16)
    incoming = cross_groups(outgoing)
    rows_in = incoming[:, :, 0].reshape(row_total, slice_width)
    rows_back = incoming[:, :, 1].reshape(row_total, slice_width)
    gate_part = jnp.dot(rows_in, w_gate, preferred_element_type=jnp.float32)
    up_part = jnp.dot(rows_in, w_up, preferred_element_type=jnp.float32)
    stacked = jnp.concatenate([gate_part, up_part], 1)
    back_part = jnp.einsum("rd,fd->rf", rows_back, w_down, preferred_element_type=jnp.float32)
    summed = whole_sum(stacked, bit_count)
    gate_pre = summed[:, :hidden_units]
    up_pre = summed[:, hidden_units:]
    hidden = activate(gate_pre, up_pre)
    d_hidden = whole_sum(back_part, bit_count)
    d_gate, d_up = gate_grads(gate_pre, up_pre, d_hidden)
    output = jnp.dot(hidden, w_down, preferred_element_type=jnp.float32).astype(jnp.bfloat16)
    grad_in = jnp.einsum("rf,df->rd", d_gate, w_gate, preferred_element_type=jnp.float32)
    grad_in = (
        grad_in + jnp.einsum("rf,df->rd", d_up, w_up, preferred_element_type=jnp.float32)
    ).astype(jnp.bfloat16)
    returned = jnp.stack([output, grad_in], 1).reshape(group_count, slot_count, 2, slice_width)
    arrived = cross_groups(returned)
    weighted = jnp.where(placed, weight_pair[:, :, None], jnp.zeros((), jnp.bfloat16))
    partial_sums = jnp.einsum(
        "tgc,gckd->tkd", weighted, arrived, preferred_element_type=jnp.float32
    )
    home = lax.all_to_all(partial_sums, "local", split_axis=0, concat_axis=0, tiled=True)
    home = jnp.sum(home.reshape(per_group, SLICES, token_count, 2, slice_width), axis=0)
    home = jnp.transpose(home, (1, 2, 0, 3)).reshape(token_count, 2, SLICES * slice_width)
    return (home[:, 0].astype(jnp.bfloat16), home[:, 1].astype(jnp.bfloat16))


def solution(mesh):
    return jax.shard_map(
        per_device,
        mesh=mesh,
        in_specs=(
            P(("group", "local"), None),
            P(("group", "local"), None),
            P(("group", "local"), None),
            P(("group", "local"), None),
            P(),
            P(("group", "local"), None),
            P(("group", "local"), None),
            P(None, ("group", "local")),
        ),
        out_specs=(P(("group", "local"), None), P(("group", "local"), None)),
        check_vma=False,
    )
```

profile of v0, /device:TPU:1, one launch (start us, length us, event | category | flops | bytes accessed | tf_op | source)
XLA Modules:
  0.0 353.6 jit_solution(526734313166897972)
XLA Ops:
  0.6 0.0 copy-start
  0.6 1.4 broadcast_in_dim.40
  2.0 14.0 %all-to-all-start = ((s32[64,2,8]{2,1,0:T(2,128)}), s32[64,2,8]{2,1,0:T(2,128)S(1)}, u32[]{:S(2)}, u32[]{:S(2)}) async-start(s32[64,2,8]{2,1,0:T(2,128)} %broadcast_in_dim.40), calls=%async_computation | async-start | bytes 131072 | tf_op jit(solution)/shard_map/all_to_all | solution.py:76
  16.1 0.7 copy_bitcast_fusion
  16.9 0.8 select_reduce_fusion
  17.7 9.4 %all-to-all-done = s32[64,2,8]{2,1,0:T(2,128)S(1)} async-done(((s32[64,2,8]{2,1,0:T(2,128)}), s32[64,2,8]{2,1,0:T(2,128)S(1)}, u32[]{:S(2)}, u32[]{:S(2)}) %all-to-all-start) | async-done | bytes 4128 | tf_op jit(solution)/shard_map/all_to_all | solution.py:76
  27.2 0.8 broadcast_in_dim.76
  28.0 4.6 %all-to-all-start.2 = ((bf16[128,2,512]{2,1,0:T(2,128)(2,1)}), bf16[128,2,512]{2,1,0:T(2,128)(2,1)S(1)}, u32[]{:S(2)}, u32[]{:S(2)}) async-start(bf16[128,2,512]{2,1,0:T(2,128)(2,1)} %bitcast.6), calls=%async_computation.2 | async-start | bytes 524288 | tf_op jit(solution)/shard_map/all_to_all | solution.py:74
  32.7 0.1 compare_reduce_fusion
  32.8 0.1 copy.53
  32.9 0.2 reduce_window_sum.11
  33.1 0.1 copy.55
  33.2 0.1 copy.54
  33.3 11.8 %all-to-all-done.2 = bf16[128,2,512]{2,1,0:T(2,128)(2,1)S(1)} async-done(((bf16[128,2,512]{2,1,0:T(2,128)(2,1)}), bf16[128,2,512]{2,1,0:T(2,128)(2,1)S(1)}, u32[]{:S(2)}, u32[]{:S(2)}) %all-to-all-start.2) | async-done | bytes 262176 | tf_op jit(solution)/shard_map/all_to_all | solution.py:74
  45.1 0.2 convolution_convert_fusion
  45.3 0.0 copy-start.3
  45.4 0.3 copy.59
  45.7 33.0 %all_to_all.32 = bf16[16,10,2,512]{3,2,1,0:T(2,128)(2,1)S(1)} all-to-all(bf16[16,10,2,512]{3,2,1,0:T(2,128)(2,1)S(1)} %copy.59), channel_id=1, replica_groups=mesh['group'=16,'local'=64] {'group'}, dimensions={0} | all-to-all | bytes 655360 | tf_op jit(solution)/shard_map/all_to_all | solution.py:24
  78.8 2.2 slice_reduce_fusion
  80.9 1.1 reshape_squeeze.6
  82.0 0.3 fusion.29
  82.4 0.3 fusion.28
  82.7 0.1 pad_maximum_fusion
  82.8 2.5 collective-permute-start
  85.4 29.9 %collective-permute-done = f32[160,2048]{1,0:T(8,128)S(1)} collective-permute-done((f32[160,2048]{1,0:T(8,128)S(1)}, f32[160,2048]{1,0:T(8,128)S(1)}, u32[]{:S(2)}, u32[]{:S(2)}) %collective-permute-start) | collective-permute-done | bytes 1310752 | tf_op jit(solution)/shard_map/ppermute | solution.py:16
  115.3 0.2 fusion.27
  115.5 2.8 collective-permute-start.1
  118.3 1.7 reshape_squeeze.7
  120.0 1.4 fusion.30
  121.4 2.4 collective-permute-start.3
  123.8 53.0 %collective-permute-done.1 = f32[160,2048]{1,0:T(8,128)} collective-permute-done((f32[160,2048]{1,0:T(8,128)S(1)}, f32[160,2048]{1,0:T(8,128)}, u32[]{:S(2)}, u32[]{:S(2)}) %collective-permute-start.1) | collective-permute-done | bytes 1310752 | tf_op jit(solution)/shard_map/ppermute | solution.py:16
  176.9 1.8 add.46
  178.7 3.4 collective-permute-start.2
  182.1 0.0 collective-permute-done.3
  182.1 0.1 add.49
  182.2 0.0 copy-start.5
  182.2 1.9 collective-permute-start.4
  184.2 84.4 %collective-permute-done.4 = f32[160,1024]{1,0:T(8,128)S(1)} collective-permute-done((f32[160,1024]{1,0:T(8,128)S(1)}, f32[160,1024]{1,0:T(8,128)S(1)}, u32[]{:S(2)}, u32[]{:S(2)}) %collective-permute-start.4) | collective-permute-done | bytes 655392 | tf_op jit(solution)/shard_map/ppermute | solution.py:16
  268.6 1.0 add.50
  269.6 4.1 %collective-permute-start.5 = (f32[160,1024]{1,0:T(8,128)}, f32[160,1024]{1,0:T(8,128)}, u32[]{:S(2)}, u32[]{:S(2)}) collective-permute-start(f32[160,1024]{1,0:T(8,128)} %add.50), channel_id=1, source_target_pairs={{0,4},{4,0},{1,5},{5,1},{2,6},{6,2},{3,7},{7,3},{8,12},{12,8},{9,1... | collective-permute-start | bytes 1966088 | tf_op jit(solution)/shard_map/ppermute | solution.py:16
  273.7 0.6 broadcast_in_dim.70
  274.3 6.1 %all-to-all-start.1 = ((bf16[64,2,8]{2,1,0:T(2,128)(2,1)}), bf16[64,2,8]{2,1,0:T(2,128)(2,1)S(1)}, u32[]{:S(2)}, u32[]{:S(2)}) async-start(bf16[64,2,8]{2,1,0:T(2,128)(2,1)} %broadcast_in_dim.70), calls=%async_computation.1 | async-start | bytes 65536 | tf_op jit(solution)/shard_map/all_to_all | solution.py:75
  280.4 0.0 collective-permute-done.2
  280.5 1.5 add.47
  281.9 0.4 convolution_convert_fusion.1
  282.3 0.0 copy-start.4
  282.3 23.5 %collective-permute-done.5 = f32[160,1024]{1,0:T(8,128)} collective-permute-done((f32[160,1024]{1,0:T(8,128)}, f32[160,1024]{1,0:T(8,128)}, u32[]{:S(2)}, u32[]{:S(2)}) %collective-permute-start.5) | collective-permute-done | bytes 655392 | tf_op jit(solution)/shard_map/ppermute | solution.py:16
  305.8 1.9 fusion.3
  307.7 0.0 copy-done.4
  307.7 1.8 fusion
  309.6 0.1 stack.22
  309.6 0.1 stack.21
  309.7 0.1 pad_maximum_fusion.1
  309.8 1.1 copy.60
  310.8 0.0 all-to-all-done.1
  310.8 3.9 %all-to-all-start.4 = ((bf16[16,10,2,512]{3,2,1,0:T(2,128)(2,1)}), bf16[16,10,2,512]{3,2,1,0:T(2,128)(2,1)S(1)}, u32[]{:S(2)}, u32[]{:S(2)}) async-start(bf16[16,10,2,512]{3,2,1,0:T(2,128)(2,1)} %copy.60), calls=%async_computation.4 | async-start | bytes 655360 | tf_op jit(solution)/shard_map/all_to_all | solution.py:24
  314.7 0.1 copy.56
  314.8 0.1 fusion.20
  314.9 12.9 %all-to-all-done.4 = bf16[16,10,2,512]{3,2,1,0:T(2,128)(2,1)S(1)} async-done(((bf16[16,10,2,512]{3,2,1,0:T(2,128)(2,1)}), bf16[16,10,2,512]{3,2,1,0:T(2,128)(2,1)S(1)}, u32[]{:S(2)}, u32[]{:S(2)}) %all-to-all-start.4) | async-done | bytes 327712 | tf_op jit(solution)/shard_map/all_to_all | solution.py:24
  327.8 0.2 convolution_bitcast_fusion
  328.0 0.4 copy.62
  328.4 24.3 %all_to_all.33 = f32[128,2,512]{2,1,0:T(2,128)S(1)} all-to-all(f32[128,2,512]{2,1,0:T(2,128)S(1)} %copy.62), channel_id=1, replica_groups=mesh['group'=16,'local'=64] {'local'}, dimensions={0} | all-to-all | bytes 1048576 | tf_op jit(solution)/shard_map/all_to_all | solution.py:124
  352.8 0.2 reduce_sum.32
  353.0 0.6 slice_bitcast_fusion
  (15 shorter events, 0.2 us)
Async XLA Ops:
  0.6 119.3 %copy-start = (bf16[1024,512]{1,0:T(8,128)(2,1)S(1)}, bf16[1024,512]{1,0:T(8,128)(2,1)}, u32[]{:S(2)}) copy-start(bf16[1024,512]{1,0:T(8,128)(2,1)} %param.15) | copy-start | bytes 3145732
  2.0 25.1 %all-to-all-start = ((s32[64,2,8]{2,1,0:T(2,128)}), s32[64,2,8]{2,1,0:T(2,128)S(1)}, u32[]{:S(2)}, u32[]{:S(2)}) async-start(s32[64,2,8]{2,1,0:T(2,128)} %broadcast_in_dim.40), calls=%async_computation | async-start | bytes 131072 | tf_op jit(solution)/shard_map/all_to_all | solution.py:76
  28.0 17.1 %all-to-all-start.2 = ((bf16[128,2,512]{2,1,0:T(2,128)(2,1)}), bf16[128,2,512]{2,1,0:T(2,128)(2,1)S(1)}, u32[]{:S(2)}, u32[]{:S(2)}) async-start(bf16[128,2,512]{2,1,0:T(2,128)(2,1)} %bitcast.6), calls=%async_computation.2 | async-start | bytes 524288 | tf_op jit(solution)/shard_map/all_to_all | solution.py:74
  45.3 36.7 %copy-start.3 = (bf16[512,1024]{1,0:T(8,128)(2,1)S(1)}, bf16[512,1024]{1,0:T(8,128)(2,1)}, u32[]{:S(2)}) copy-start(bf16[512,1024]{1,0:T(8,128)(2,1)} %param.14) | copy-start | bytes 3145732
  80.9 1.5 copy-start.2
  82.8 32.5 %collective-permute-start = (f32[160,2048]{1,0:T(8,128)S(1)}, f32[160,2048]{1,0:T(8,128)S(1)}, u32[]{:S(2)}, u32[]{:S(2)}) collective-permute-start(f32[160,2048]{1,0:T(8,128)S(1)} %pad_maximum_fusion), channel_id=1, source_target_pairs={{0,1},{1,0},{2,3},{3,2},{4,5},{5,4},{6,7},{7,6},{8,9},{9,8},{10,11... | collective-permute-start | bytes 3932168 | tf_op jit(solution)/shard_map/ppermute | solution.py:16
  115.5 8.3 %copy-start.1 = (f32[160,2048]{1,0:T(8,128)}, f32[160,2048]{1,0:T(8,128)S(1)}, u32[]{:S(2)}) copy-start(f32[160,2048]{1,0:T(8,128)S(1)} %fusion.27) | copy-start | bytes 3932164
  115.5 61.4 %collective-permute-start.1 = (f32[160,2048]{1,0:T(8,128)S(1)}, f32[160,2048]{1,0:T(8,128)}, u32[]{:S(2)}, u32[]{:S(2)}) collective-permute-start(f32[160,2048]{1,0:T(8,128)S(1)} %fusion.27), channel_id=1, source_target_pairs={{0,2},{2,0},{1,3},{3,1},{4,6},{6,4},{5,7},{7,5},{8,10},{10,8},{9,1... | collective-permute-start | bytes 3932168 | tf_op jit(solution)/shard_map/ppermute | solution.py:16
  121.4 60.8 %collective-permute-start.3 = (f32[160,1024]{1,0:T(8,128)S(1)}, f32[160,1024]{1,0:T(8,128)S(1)}, u32[]{:S(2)}, u32[]{:S(2)}) collective-permute-start(f32[160,1024]{1,0:T(8,128)S(1)} %fusion.30), channel_id=1, source_target_pairs={{0,1},{1,0},{2,3},{3,2},{4,5},{5,4},{6,7},{7,6},{8,9},{9,8},{10,11... | collective-permute-start | bytes 1966088 | tf_op jit(solution)/shard_map/ppermute | solution.py:16
  178.7 101.7 %collective-permute-start.2 = (f32[160,2048]{1,0:T(8,128)S(1)}, f32[160,2048]{1,0:T(8,128)}, u32[]{:S(2)}, u32[]{:S(2)}) collective-permute-start(f32[160,2048]{1,0:T(8,128)S(1)} %add.46), channel_id=1, source_target_pairs={{0,4},{4,0},{1,5},{5,1},{2,6},{6,2},{3,7},{7,3},{8,12},{12,8},{9,1... | collective-permute-start | bytes 3932168 | tf_op jit(solution)/shard_map/ppermute | solution.py:16
  182.2 91.4 %copy-start.5 = (bf16[2,8]{1,0:T(2,128)(2,1)S(1)}, bf16[2,8]{1,0:T(2,128)(2,1)}, u32[]{:S(2)}) copy-start(bf16[2,8]{1,0:T(2,128)(2,1)} %param.10) | copy-start | bytes 100
  182.2 86.4 %collective-permute-start.4 = (f32[160,1024]{1,0:T(8,128)S(1)}, f32[160,1024]{1,0:T(8,128)S(1)}, u32[]{:S(2)}, u32[]{:S(2)}) collective-permute-start(f32[160,1024]{1,0:T(8,128)S(1)} %add.49), channel_id=1, source_target_pairs={{0,2},{2,0},{1,3},{3,1},{4,6},{6,4},{5,7},{7,5},{8,10},{10,8},{9,1... | collective-permute-start | bytes 1966088 | tf_op jit(solution)/shard_map/ppermute | solution.py:16
  269.6 36.2 %collective-permute-start.5 = (f32[160,1024]{1,0:T(8,128)}, f32[160,1024]{1,0:T(8,128)}, u32[]{:S(2)}, u32[]{:S(2)}) collective-permute-start(f32[160,1024]{1,0:T(8,128)} %add.50), channel_id=1, source_target_pairs={{0,4},{4,0},{1,5},{5,1},{2,6},{6,2},{3,7},{7,3},{8,12},{12,8},{9,1... | collective-permute-start | bytes 1966088 | tf_op jit(solution)/shard_map/ppermute | solution.py:16
  274.3 36.5 %all-to-all-start.1 = ((bf16[64,2,8]{2,1,0:T(2,128)(2,1)}), bf16[64,2,8]{2,1,0:T(2,128)(2,1)S(1)}, u32[]{:S(2)}, u32[]{:S(2)}) async-start(bf16[64,2,8]{2,1,0:T(2,128)(2,1)} %broadcast_in_dim.70), calls=%async_computation.1 | async-start | bytes 65536 | tf_op jit(solution)/shard_map/all_to_all | solution.py:75
  282.3 25.4 %copy-start.4 = (bf16[512,1024]{1,0:T(8,128)(2,1)S(1)}, bf16[512,1024]{1,0:T(8,128)(2,1)}, u32[]{:S(2)}) copy-start(bf16[512,1024]{1,0:T(8,128)(2,1)} %param.14) | copy-start | bytes 3145732
  310.8 16.9 %all-to-all-start.4 = ((bf16[16,10,2,512]{3,2,1,0:T(2,128)(2,1)}), bf16[16,10,2,512]{3,2,1,0:T(2,128)(2,1)S(1)}, u32[]{:S(2)}, u32[]{:S(2)}) async-start(bf16[16,10,2,512]{3,2,1,0:T(2,128)(2,1)} %copy.60), calls=%async_computation.4 | async-start | bytes 655360 | tf_op jit(solution)/shard_map/all_to_all | solution.py:24
where the time goes:
time: 355 us; the launch traced here: 354 us
  waiting for transfers between devices  225 us (63%)
  blocking collectives  57.4 us (16%)
  starting transfers between devices  45.8 us (13%)
  local copies, waits for them, and re-layouts  11.6 us (3%)
  matrix products  6.69 us (2%)
  other arithmetic  6.21 us (2%)
    ppermute x6, waiting for transfers between devices, from_partner(): return lax.ppermute(block, axis, route)  191 us
    all_to_all x1, blocking collectives, cross_groups(): lax.all_to_all(values, 'group', split_axis=0, concat_axis=0, tiled=True)  33 us
    all_to_all x1, blocking collectives, per_device(): lax.all_to_all(partial_sums, 'local', split_axis=0, concat_axis=0, tiled=...  24.3 us
    ppermute x6, starting transfers between devices, from_partner(): return lax.ppermute(block, axis, route)  17.1 us
    all_to_all x1, starting transfers between devices, per_device(): lax.all_to_all(send_ids, 'local', split_axis=0, concat_axis=0, tiled=True)  14 us
    all_to_all x1, waiting for transfers between devices, cross_groups(): lax.all_to_all(values, 'group', split_axis=0, concat_axis=0, tiled=True)  12.9 us
    all_to_all x1, waiting for transfers between devices, per_device(): lax.all_to_all(send_rows, 'local', split_axis=0, concat_axis=0, tiled=True)  11.8 us
    all_to_all x1, waiting for transfers between devices, per_device(): lax.all_to_all(send_ids, 'local', split_axis=0, concat_axis=0, tiled=True)  9.42 us
  transfers between devices with their start and end apart: 10, of which 7 were waited for; matrix products, arithmetic and copies ran while one was open for 4% of the time, Pallas kernels for 0%

commit v1 on v0

v1 whole, which is shorter than its diff:
```python
import functools

import jax
import jax.numpy as jnp
from jax import lax
from jax.experimental import pallas as pl
from jax.experimental.pallas import tpu as pltpu
from jax.sharding import PartitionSpec as P

LANES = 128
BF16 = jnp.bfloat16
F32 = jnp.float32
MESH = pl.DeviceIdType.MESH
CONTRACT_LAST = (((1,), (1,)), ((), ()))


def matmul(a, b):
    return jnp.dot(a, b, preferred_element_type=F32)


def matmul_t(a, b):
    return lax.dot_general(a, b, CONTRACT_LAST, preferred_element_type=F32)


def moe_kernel(
    nx, ny, ng, slots,
    tokens, cotangent, gates, ids, cap, wg_hbm, wu_hbm, wd_hbm,
    mixed, token_grad,
    wg, wu, wd, meta2, xs_f, xs, xr, xf, yb, wsel_t, rows_f, zs, zr, acts,
    rs_out, rs_in, hid, acc, ps, pf, ys, yr, xo, xi, final,
    w_sem, x_sem, y_sem, z_sem, rs_sem, ag_sem, r_sem, ys_sem, xo_sem,
):
    tok, width = tokens.shape
    top = ids.shape[1]
    w = wg.shape[0]
    fc = wg.shape[1] // nx
    nj = w // LANES
    ns = 2 * nj
    block = nx * tok
    group = ny * block
    rows = ng * slots
    half = rows // 2
    used = slots * nj
    padded = zs.shape[3]
    hx, hy = nx // 2, ny // 2

    g = lax.axis_index("group")
    at = lax.axis_index("local")
    y = lax.div(at, nx)
    x = lax.rem(at, nx)

    def x_dev(k):
        return {"local": y * nx + lax.rem(x + k + nx, nx)}

    def y_dev(k):
        return {"local": lax.rem(y + k + ny, ny) * nx + x}

    def g_dev(k):
        return {"group": lax.rem(g + k, ng)}

    def each(low, high, body):
        def step(i, carry):
            body(i)
            return carry
        lax.fori_loop(low, high, step, 0)

    def remote(src, dst, sems, index, device):
        return pltpu.make_async_remote_copy(
            src_ref=src, dst_ref=dst, send_sem=sems.at[(0,) + index], recv_sem=sems.at[(1,) + index],
            device_id=device, device_id_type=MESH)

    weights = [pltpu.make_async_copy(a, b, w_sem.at[i])
               for i, (a, b) in enumerate(((wg_hbm, wg), (wu_hbm, wu), (wd_hbm, wd)))]
    for copy in weights:
        copy.start()

    barrier = pltpu.get_barrier_semaphore()

    def greet(device):
        pl.semaphore_signal(barrier, inc=1, device_id=device, device_id_type=MESH)

    each(1, nx, lambda k: greet(x_dev(k)))
    each(1, ny, lambda k: greet(y_dev(k)))
    each(1, ng, lambda k: greet(g_dev(k)))

    meta2[...] = jnp.zeros_like(meta2)
    meta2[:, 0:top] = ids[...].astype(F32)
    meta2[:, top:2 * top] = gates[...].astype(F32)
    xs_f[...] = jnp.zeros_like(xs_f)

    def cut(dest):
        start = pl.multiple_of(dest * w, LANES)
        for side, ref in enumerate((tokens, cotangent)):
            v = ref[:, pl.ds(start, w)].astype(F32)
            for i in range(tok):
                for j in range(nj):
                    r = i * ns + side * nj + j
                    xs_f[dest, r:r + 1, :] = v[i:i + 1, j * LANES:(j + 1) * LANES]
        for i in range(tok):
            r = tok * ns + i * ns
            xs_f[dest, r:r + 1, :] = meta2[i:i + 1, :]

    each(0, nx, cut)
    xs[...] = xs_f[...].astype(BF16)
    xr[pl.ds(x, 1)] = xs[pl.ds(x, 1)]
    pl.semaphore_wait(barrier, nx + ny + ng - 3)

    def x_copy(k, peer):
        return remote(xs.at[lax.rem(x + k, nx)], xr.at[peer], x_sem, (k,), x_dev(k))

    each(1, nx, lambda k: x_copy(k, x).start())
    each(1, nx, lambda k: x_copy(k, lax.rem(x - k + nx, nx)).wait_recv())

    tr = tok * ns
    xf[0] = xr[:, 0:tr].astype(F32).reshape(nx * tr, LANES)
    xf[1] = xr[:, tr:2 * tr].astype(F32).reshape(nx * tr, LANES)
    for s in range(ns):
        yb[y, s] = xf[0, pl.ds(s, block, stride=ns), :].astype(BF16)
    yb[y, ns] = xf[1, pl.ds(0, block, stride=ns), :].astype(BF16)

    cut_y = (ns + 1) // 2

    def y_part(chunk, direction, k):
        ref = yb.at[chunk]
        if k < hy:
            return ref
        return ref.at[pl.ds(0, cut_y)] if direction == 0 else ref.at[pl.ds(cut_y, ns + 1 - cut_y)]

    def y_copy(direction, k, receive=False):
        sign = 1 if direction == 0 else -1
        back = k if receive else k - 1
        chunk = lax.rem(y - sign * back + ny, ny)
        ref = y_part(chunk, direction, k)
        return remote(ref, ref, y_sem, (direction, k), y_dev(sign))

    for k in range(1, hy + 1):
        for direction in range(2):
            if k > 1:
                y_copy(direction, k - 1, True).wait_recv()
            y_copy(direction, k).start()
    for direction in range(2):
        y_copy(direction, hy, True).wait_recv()

    meta = yb[:, ns].astype(F32).reshape(group, LANES)
    expert = lax.broadcasted_iota(jnp.int32, (group, LANES), 1).astype(F32)
    hit = jnp.zeros((group, LANES), F32)
    weight = jnp.zeros((group, LANES), F32)
    for k in range(top):
        same = meta[:, k:k + 1] == expert
        hit = jnp.where(same, 1.0, hit)
        weight = jnp.where(same, meta[:, top + k:top + k + 1], weight)
    earlier = (lax.broadcasted_iota(jnp.int32, (group, group), 1)
               < lax.broadcasted_iota(jnp.int32, (group, group), 0))
    rank = matmul(jnp.where(earlier, 1.0, 0.0).astype(BF16), hit.astype(BF16))
    kept = (hit > 0.5) & (rank < cap[...].astype(F32))
    rank = jnp.where(kept, rank, -1.0).astype(BF16)
    weight = weight.astype(BF16)

    r_group = jnp.floor((lax.broadcasted_iota(jnp.int32, (rows, LANES), 0).astype(F32) + 0.5) * (1.0 / slots))
    r_expert = r_group * ny + y.astype(F32)
    pick = jnp.where(lax.broadcasted_iota(jnp.int32, (rows, LANES), 1).astype(F32) == r_expert, 1.0, 0.0).astype(BF16)
    r_at = lax.broadcasted_iota(jnp.int32, (rows, group), 0).astype(F32)
    r_slot = r_at - jnp.floor((r_at + 0.5) * (1.0 / slots)) * slots
    select = jnp.where(matmul_t(pick, rank) == r_slot, 1.0, 0.0).astype(BF16)
    c_at = lax.broadcasted_iota(jnp.int32, (group, rows), 1).astype(F32)
    c_slot = c_at - jnp.floor((c_at + 0.5) * (1.0 / slots)) * slots
    wsel_t[...] = jnp.where(matmul_t(rank, pick) == c_slot, matmul_t(weight, pick), 0.0).astype(BF16)

    def spread(side, way):
        def one(k):
            dest = lax.rem(g + k, ng)
            part = rows_f[side, pl.ds(pl.multiple_of(dest * used, 8), used), :]
            if padded > used:
                part = jnp.concatenate([part, jnp.zeros((padded - used, LANES), F32)], 0)
            return dest, part.astype(BF16)

        def go(k):
            dest, part = one(k)
            zs[way, side, dest] = part
            z_copy(way, side, k, g).start()

        dest, part = one(0)
        zr[way, side, dest] = part
        each(1, ng, go)

    def z_copy(way, side, k, peer):
        return remote(zs.at[way, side, lax.rem(g + k, ng)], zr.at[way, side, peer],
                      z_sem, (way, side, k), g_dev(k))

    def collect(way, side):
        each(1, ng, lambda k: z_copy(way, side, k, lax.rem(g - k + ng, ng)).wait_recv())
        got = zr[way, side].astype(F32)
        rows_f[2 + side] = got[:, 0:used].reshape(ng * used, LANES)
        return [rows_f[2 + side, pl.ds(j, rows, stride=nj), :].astype(BF16) for j in range(nj)]

    for side in range(2):
        for j in range(nj):
            held = yb[:, side * nj + j].reshape(group, LANES)
            rows_f[side, pl.ds(j, rows, stride=nj), :] = matmul(select, held)
        spread(side, 0)

    def lanes_of(chunk):
        return pl.ds(pl.multiple_of(chunk * fc, LANES), fc)

    def products(kind, chunk):
        here = lanes_of(chunk)
        if kind == 0:
            both = matmul(acts[0], jnp.concatenate([wg[:, here], wu[:, here]], 1))
            return [(0, both[:, 0:fc]), (1, both[:, fc:2 * fc])]
        return [(2, matmul_t(acts[1], wd[here, :]))]

    def span(direction, far):
        return pl.ds(0, rows) if not far else pl.ds(0, half) if direction == 0 else pl.ds(half, rows - half)

    def rs_copy(direction, d, m):
        part = span(direction, d == hx)
        return remote(rs_out.at[direction, d - 1, m, part], rs_in.at[direction, d - 1, m, part],
                      rs_sem, (direction, d - 1, m), x_dev(1 if direction == 0 else -1))

    def rs_step(kind, d):
        shared = products(kind, lax.rem(x + hx, nx)) if d == hx else None
        for direction in range(2):
            sign = 1 if direction == 0 else -1
            mine = shared if d == hx else products(kind, lax.rem(x + sign * d + nx, nx))
            for m, part in mine:
                if d == hx:
                    p = span(direction, True)
                    rs_out[direction, d - 1, m, p] = part[0:half].astype(BF16) if direction == 0 else part[half:rows].astype(BF16)
                else:
                    rs_copy(direction, d + 1, m).wait_recv()
                    if d + 1 == hx:
                        add = rs_in[direction, d, m, span(direction, True)].astype(F32)
                        if direction == 0:
                            part = jnp.concatenate([part[0:half] + add, part[half:rows]], 0)
                        else:
                            part = jnp.concatenate([part[0:half], part[half:rows] + add], 0)
                    else:
                        part = part + rs_in[direction, d, m].astype(F32)
                    rs_out[direction, d - 1, m] = part.astype(BF16)
                rs_copy(direction, d, m).start()

    def rs_last(kind):
        totals = []
        for m, part in products(kind, x):
            for direction in range(2):
                rs_copy(direction, 1, m).wait_recv()
                part = part + rs_in[direction, 0, m].astype(F32)
            totals.append(part)
        return totals

    def ag_copy(direction, k, m, receive=False):
        sign = 1 if direction == 0 else -1
        back = k if receive else k - 1
        chunk = lax.rem(x - sign * back + nx, nx)
        ref = hid.at[chunk, m, span(direction, k == hx)]
        return remote(ref, ref, ag_sem, (direction, k - 1, m), x_dev(sign))

    def ag_step(m, k):
        for direction in range(2):
            if k > 1:
                ag_copy(direction, k - 1, m, True).wait_recv()
            ag_copy(direction, k, m).start()

    def add_out(chunk):
        acc[0] += matmul(hid[chunk, 0], wd[lanes_of(chunk), :])

    def add_grad(chunk):
        here = lanes_of(chunk)
        acc[1] += matmul_t(jnp.concatenate([hid[chunk, 1], hid[chunk, 2]], 1),
                           jnp.concatenate([wg[:, here], wu[:, here]], 1))

    for j, part in enumerate(collect(0, 0)):
        acts[0, :, j * LANES:(j + 1) * LANES] = part
    for copy in weights:
        copy.wait()
    rs_step(0, hx)
    for j, part in enumerate(collect(0, 1)):
        acts[1, :, j * LANES:(j + 1) * LANES] = part
    for d in range(hx - 1, 0, -1):
        rs_step(0, d)
        rs_step(1, d + 1)
    gate_pre, up_pre = rs_last(0)
    sig = jax.nn.sigmoid(gate_pre)
    silu = gate_pre * sig
    hid[x, 0] = (silu * up_pre).astype(BF16)
    ag_step(0, 1)
    d_gate_by = up_pre * sig * (1.0 + gate_pre * (1.0 - sig))
    rs_step(1, 1)
    acc[...] = jnp.zeros_like(acc)
    add_out(x)
    (d_hidden,) = rs_last(1)
    hid[x, 1] = (d_hidden * d_gate_by).astype(BF16)
    hid[x, 2] = (d_hidden * silu).astype(BF16)
    ag_step(1, 1)
    ag_step(2, 1)
    add_grad(x)

    def left(k):
        return lax.rem(x - k + nx, nx)

    def right(k):
        return lax.rem(x + k, nx)

    def send_back(side):
        for j in range(nj):
            rows_f[side, pl.ds(j, rows, stride=nj), :] = acc[side, :, j * LANES:(j + 1) * LANES]
        spread(side, 1)

    for k in range(2, hx + 1):
        ag_step(0, k)
        add_out(left(k - 1))
        add_out(right(k - 1))
        if k > 2:
            ag_step(1, k - 1)
            ag_step(2, k - 1)
            add_grad(left(k - 2))
            add_grad(right(k - 2))
    for direction in range(2):
        ag_copy(direction, hx, 0, True).wait_recv()
    add_out(right(hx))
    send_back(0)
    ag_step(1, hx)
    ag_step(2, hx)
    add_grad(left(hx - 1))
    add_grad(right(hx - 1))
    for m in (1, 2):
        for direction in range(2):
            ag_copy(direction, hx, m, True).wait_recv()
    add_grad(right(hx))
    send_back(1)

    def ys_copy(side, k, peer):
        return remote(ys.at[side, lax.rem(y + k, ny)], yr.at[side, peer], ys_sem, (side, k), y_dev(k))

    def xo_copy(side, k, peer):
        dest = lax.rem(x + k, nx)
        return remote(xo.at[side, dest], xi.at[side, peer], xo_sem, (side, k), x_dev(k))

    def home_rows(side):
        for j, part in enumerate(collect(1, side)):
            total = matmul(wsel_t[...], part)
            pf[j] = total
            ys[side, :, j] = total.astype(BF16).reshape(ny, block, LANES)
        each(1, ny, lambda k: ys_copy(side, k, y).start())

    def home_sum(side):
        each(1, ny, lambda k: ys_copy(side, k, lax.rem(y - k + ny, ny)).wait_recv())
        for j in range(nj):
            total = ps[side, j]
            for k in range(1, ny):
                total = total + yr[side, lax.rem(y + k, ny), j].astype(F32)
            final[pl.ds(j, block, stride=nj), :] = total
        xo[side] = final[...].reshape(nx, tok * nj, LANES)
        xi[side, pl.ds(x, 1)] = xo[side, pl.ds(x, 1)]
        each(1, nx, lambda k: xo_copy(side, k, x).start())

    def keep_own(side):
        for j in range(nj):
            ps[side, j] = pf[j, pl.ds(pl.multiple_of(y * block, 8), block), :]

    def finish(side, out):
        each(1, nx, lambda k: xo_copy(side, k, lax.rem(x - k + nx, nx)).wait_recv())
        whole = []
        for src in range(nx):
            got = xi[side, src]
            for j in range(nj):
                whole.append(jnp.concatenate([got[i * nj + j:i * nj + j + 1] for i in range(tok)], 0))
        out[...] = jnp.concatenate(whole, 1).astype(BF16)

    home_rows(0)
    keep_own(0)
    home_sum(0)
    home_rows(1)
    keep_own(1)
    home_sum(1)
    finish(0, mixed)
    finish(1, token_grad)

    each(1, nx, lambda k: x_copy(k, x).wait_send())
    for direction in range(2):
        for k in range(1, hy + 1):
            y_copy(direction, k).wait_send()
        for d in range(1, hx + 1):
            for m in range(3):
                rs_copy(direction, d, m).wait_send()
                ag_copy(direction, d, m).wait_send()
    for side in range(2):
        for way in range(2):
            each(1, ng, lambda k: z_copy(way, side, k, g).wait_send())
        each(1, ny, lambda k: ys_copy(side, k, y).wait_send())
        each(1, nx, lambda k: xo_copy(side, k, x).wait_send())


def per_device(nx, ny, ng, tokens, cotangent, gates, expert_ids, capacity, w_gate, w_up, w_down):
    tok, width = tokens.shape
    top = expert_ids.shape[1]
    w, ff = w_gate.shape
    experts = capacity.shape[0]
    block = nx * tok
    group = ny * block
    slots = min(group * top // experts * 5 // 4, group)
    rows = ng * slots
    nj = w // LANES
    ns = 2 * nj
    fc = ff // nx
    padded = -(-slots * nj // 16) * 16
    cap = capacity.reshape(1, experts)
    if experts < LANES:
        cap = jnp.pad(cap, ((0, 0), (0, LANES - experts)))
    vmem = pl.BlockSpec(memory_space=pltpu.VMEM)
    hbm = pl.BlockSpec(memory_space=pl.ANY)
    dma = pltpu.SemaphoreType.DMA
    return pl.pallas_call(
        functools.partial(moe_kernel, nx, ny, ng, slots),
        out_shape=[jax.ShapeDtypeStruct((tok, width), BF16)] * 2,
        in_specs=[vmem] * 5 + [hbm] * 3,
        out_specs=[vmem] * 2,
        scratch_shapes=[
            pltpu.VMEM((w, ff), BF16),
            pltpu.VMEM((w, ff), BF16),
            pltpu.VMEM((ff, w), BF16),
            pltpu.VMEM((tok, LANES), F32),
            pltpu.VMEM((nx, 2 * tok * ns, LANES), F32),
            pltpu.VMEM((nx, 2 * tok * ns, LANES), BF16),
            pltpu.VMEM((nx, 2 * tok * ns, LANES), BF16),
            pltpu.VMEM((2, nx * tok * ns, LANES), F32),
            pltpu.VMEM((ny, ns + 1, block, LANES), BF16),
            pltpu.VMEM((group, rows), BF16),
            pltpu.VMEM((4, rows * nj, LANES), F32),
            pltpu.VMEM((2, 2, ng, padded, LANES), BF16),
            pltpu.VMEM((2, 2, ng, padded, LANES), BF16),
            pltpu.VMEM((2, rows, w), BF16),
            pltpu.VMEM((2, nx // 2, 3, rows, fc), BF16),
            pltpu.VMEM((2, nx // 2, 3, rows, fc), BF16),
            pltpu.VMEM((nx, 3, rows, fc), BF16),
            pltpu.VMEM((2, rows, w), F32),
            pltpu.VMEM((2, nj, block, LANES), F32),
            pltpu.VMEM((nj, group, LANES), F32),
            pltpu.VMEM((2, ny, nj, block, LANES), BF16),
            pltpu.VMEM((2, ny, nj, block, LANES), BF16),
            pltpu.VMEM((2, nx, tok * nj, LANES), F32),
            pltpu.VMEM((2, nx, tok * nj, LANES), F32),
            pltpu.VMEM((block * nj, LANES), F32),
            dma((3,)),
            dma((2, nx)),
            dma((2, 2, ny // 2 + 1)),
            dma((2, 2, 2, ng)),
            dma((2, 2, nx // 2, 3)),
            dma((2, 2, nx // 2, 3)),
            dma((1,)),
            dma((2, 2, ny)),
            dma((2, 2, nx)),
        ],
        compiler_params=pltpu.CompilerParams(
            collective_id=0, has_side_effects=True, vmem_limit_bytes=40 * 1024 * 1024),
    )(tokens, cotangent, gates, expert_ids, cap, w_gate, w_up, w_down)


def solution(mesh):
    def run(tokens, cotangent, gates, expert_ids, capacity, w_gate, w_up, w_down):
        ng, local = mesh.shape["group"], mesh.shape["local"]
        w = w_gate.shape[0] // (ng * local)
        nx = tokens.shape[1] // w
        spec = P(("group", "local"), None)
        return jax.shard_map(
            functools.partial(per_device, nx, local // nx, ng),
            mesh=mesh,
            in_specs=(spec, spec, spec, spec, P(), spec, spec, P(None, ("group", "local"))),
            out_specs=(spec, spec),
            check_vma=False,
        )(tokens, cotangent, gates, expert_ids, capacity, w_gate, w_up, w_down)

    return run
```

time: 355 us -> 115 us (0.32)
  waiting for transfers between devices: 225 us -> 0 us
  Pallas kernels: 0 us -> 106 us
  blocking collectives: 57.4 us -> 0 us
  starting transfers between devices: 45.8 us -> 0 us
  matrix products: 6.69 us -> 0 us
  other arithmetic: 6.21 us -> 0 us
  local copies, waits for them, and re-layouts: 11.6 us -> 7.64 us
    ppermute x6 -> x0, waiting for transfers between devices: 191 us -> none  [from_partner(): return lax.ppermute(block, axis, route)]
    pallas_call x0 -> x1, Pallas kernels: none -> 106 us  [per_device(): pl.pallas_call(functools.partial(moe_kernel, nx, ny, ng, slots), out_shap...]
    all_to_all x2 -> x0, blocking collectives: 57.4 us -> none  [the longest x1 33 us: cross_groups(): lax.all_to_all(values, 'group', split_axis=0, concat_axis=0, tiled=True)]
    all_to_all x4 -> x0, waiting for transfers between devices: 34.1 us -> none  [the longest x1 12.9 us: cross_groups(): lax.all_to_all(values, 'group', split_axis=0, concat_axis=0, tiled=True)]
    all_to_all x4 -> x0, starting transfers between devices: 28.7 us -> none  [the longest x1 14 us: per_device(): lax.all_to_all(send_ids, 'local', split_axis=0, concat_axis=0, tiled=True)]
    ppermute x6 -> x0, starting transfers between devices: 17.1 us -> none  [from_partner(): return lax.ppermute(block, axis, route)]
    unnamed x13 -> x18, local copies, waits for them, and re-layouts: 0.06 us -> 7.64 us
    dot_general x8 -> x0, matrix products: 6.69 us -> none  [the longest x1 1.92 us: per_device(): jnp.einsum('rf,df->rd', d_gate, w_gate, preferred_element_type=jnp.float32)]
  transfers between devices with their start and end apart: 10 -> 0, of which waited for: 7 -> 0; matrix products, arithmetic and copies ran while one was open for 4% -> 0% of each run, Pallas kernels for 0% -> 0%
where the time goes in v1:
time: 115 us
  Pallas kernels  106 us (92%)
  local copies, waits for them, and re-layouts  7.64 us (7%)
    pallas_call x1, Pallas kernels, per_device(): pl.pallas_call(functools.partial(moe_kernel, nx, ny, ng, slots), out_shap...  106 us
    unnamed x18, local copies, waits for them, and re-layouts  7.64 us

profile of v1, /device:TPU:1, one launch (start us, length us, event | category | flops | bytes accessed | tf_op | source)
XLA Modules:
  0.0 114.8 jit_solution(9482056801126394312)
XLA Ops:
  0.6 0.0 copy-start.5
  0.6 0.0 copy-start.6
  0.7 0.7 copy-done.5
  1.3 0.0 copy-done.6
  1.3 0.0 copy-start
  1.3 1.2 %copy-done = bf16[512,1024]{1,0:T(8,128)(2,1)S(1)} copy-done((bf16[512,1024]{1,0:T(8,128)(2,1)S(1)}, bf16[512,1024]{1,0:T(8,128)(2,1)}, u32[]{:S(2)}) %copy-start) | copy-done | bytes 1048600
  2.5 0.0 copy-start.1
  2.5 1.2 %copy-done.1 = bf16[512,1024]{1,0:T(8,128)(2,1)S(1)} copy-done((bf16[512,1024]{1,0:T(8,128)(2,1)S(1)}, bf16[512,1024]{1,0:T(8,128)(2,1)}, u32[]{:S(2)}) %copy-start.1) | copy-done | bytes 1048600
  3.8 0.0 copy-start.2
  3.8 1.2 %copy-done.2 = bf16[1024,512]{1,0:T(8,128)(2,1)S(1)} copy-done((bf16[1024,512]{1,0:T(8,128)(2,1)S(1)}, bf16[1024,512]{1,0:T(8,128)(2,1)}, u32[]{:S(2)}) %copy-start.2) | copy-done | bytes 1048600
  5.0 0.0 copy-start.3
  5.0 0.7 copy-done.3
  5.7 0.0 copy-start.4
  5.7 0.7 copy-done.4
  6.4 0.0 copy-start.7
  6.4 0.7 copy-done.7
  7.1 106.5 %shard_map.95 = (bf16[2,4096]{1,0:T(2,128)(2,1)S(1)}, bf16[2,4096]{1,0:T(2,128)(2,1)S(1)}) custom-call(bf16[2,4096]{1,0:T(2,128)(2,1)S(1)} %copy-done.3, bf16[2,4096]{1,0:T(2,128)(2,1)S(1)} %copy-done.4, bf16[2,8]{1,0:T(2,128)(2,1)S(1)} %copy-done.6, s32[2,8]{1,0:T(2,128)S(1)} %copy-done.5, s32[1,128]{1,0:T(1,128)S(1)} %bitcast.1, ...), custom_call_target="tpu_custom_call" | custom-call | tf_op jit(solution)/shard_map/pallas_call | solution.py:413
  113.6 0.6 copy.12
  114.2 0.6 copy.13
Async XLA Ops:
  0.6 0.7 copy-start.5
  0.6 0.7 copy-start.6
  1.3 1.2 %copy-start = (bf16[512,1024]{1,0:T(8,128)(2,1)S(1)}, bf16[512,1024]{1,0:T(8,128)(2,1)}, u32[]{:S(2)}) copy-start(bf16[512,1024]{1,0:T(8,128)(2,1)} %wg_hbm.1) | copy-start | bytes 3145732
  2.5 1.2 %copy-start.1 = (bf16[512,1024]{1,0:T(8,128)(2,1)S(1)}, bf16[512,1024]{1,0:T(8,128)(2,1)}, u32[]{:S(2)}) copy-start(bf16[512,1024]{1,0:T(8,128)(2,1)} %wu_hbm.1) | copy-start | bytes 3145732
  3.8 1.2 %copy-start.2 = (bf16[1024,512]{1,0:T(8,128)(2,1)S(1)}, bf16[1024,512]{1,0:T(8,128)(2,1)}, u32[]{:S(2)}) copy-start(bf16[1024,512]{1,0:T(8,128)(2,1)} %wd_hbm.1) | copy-start | bytes 3145732
  5.0 0.7 copy-start.3
  5.7 0.7 copy-start.4
  6.4 0.7 copy-start.7

commit v2 on v0

v2 whole, which is shorter than its diff:
```python
import functools

import jax
import jax.numpy as jnp
from jax import lax
from jax.experimental import pallas as pl
from jax.experimental.pallas import tpu as pltpu
from jax.sharding import PartitionSpec as P

LANES = 128
BF16 = jnp.bfloat16
F32 = jnp.float32
MESH = pl.DeviceIdType.MESH
CONTRACT_LAST = (((1,), (1,)), ((), ()))


def matmul(a, b):
    return jnp.dot(a, b, preferred_element_type=F32)


def matmul_t(a, b):
    return lax.dot_general(a, b, CONTRACT_LAST, preferred_element_type=F32)


def moe_kernel(
    nx, ny, ng, slots,
    tokens_hbm, cotangent_hbm, gates_hbm, ids_hbm, cap_hbm, wg_hbm, wu_hbm, wd_hbm,
    result,
    tokens, cotangent, gates, ids, cap, wg, wu, wd,
    meta_out, meta_in, xs_f, xs, xr, xf, wsel_t, rows_f, zs, zr, acts,
    far_out, far_in, three_out, three_in, one_out, one_in, two_out, two_in, hid, acc, ho_f, ho, hi,
    load_sem, x_sem, m_sem, z_sem, rs_sem, ag_sem, h_sem,
):
    tok, width = tokens.shape
    top = ids.shape[1]
    w = wg.shape[0]
    fc = wg.shape[1] // nx
    nj = w // LANES
    ns = 2 * nj
    nl = nx * ny
    group = nl * tok
    rows = ng * slots
    half = rows // 2
    used = slots * nj
    padded = zs.shape[3]
    hx = nx // 2

    g = lax.axis_index("group")
    at = lax.axis_index("local")
    y = lax.div(at, nx)
    x = lax.rem(at, nx)

    def x_dev(k):
        return {"local": y * nx + lax.rem(x + k + nx, nx)}

    def each(low, high, body):
        def step(i, carry):
            body(i)
            return carry
        lax.fori_loop(low, high, step, 0)

    def far_first(p, n):
        return n // 2 + (p + 1) // 2 * (1 - 2 * (p % 2))

    x_order = [far_first(q, nx) for q in range(nx)]
    x_places = [lax.rem(x + k, nx) for k in x_order]

    def each_local(body):
        def line(p):
            base = lax.rem(y + ny // 2 + lax.div(p + 1, 2) * (1 - 2 * lax.rem(p, 2)), ny) * nx
            for there in x_places:
                body(base + there, there)

        each(0, ny - 1, line)
        for there in x_places[:-1]:
            body(y * nx + there, there)

    def each_group(body):
        each(0, ng - 1, lambda p: body(lax.rem(g + ng // 2 + lax.div(p + 1, 2) * (1 - 2 * lax.rem(p, 2)), ng)))

    def remote(src, dst, sems, index, device):
        return pltpu.make_async_remote_copy(
            src_ref=src, dst_ref=dst, send_sem=sems.at[(0,) + index], recv_sem=sems.at[(1,) + index],
            device_id=device, device_id_type=MESH)

    def all_of(ref, count, sems, index):
        part = ref.at[pl.ds(0, count)]
        return remote(part, part, sems, index, x_dev(1))

    loads = [pltpu.make_async_copy(a, b, load_sem.at[i]) for i, (a, b) in enumerate((
        (tokens_hbm, tokens), (cotangent_hbm, cotangent), (gates_hbm, gates), (ids_hbm, ids),
        (cap_hbm, cap), (wg_hbm, wg), (wu_hbm, wu), (wd_hbm, wd)))]
    small, weights = loads[:5], loads[5:]
    for copy in loads:
        copy.start()

    barrier = pltpu.get_barrier_semaphore()

    def greet(device):
        pl.semaphore_signal(barrier, inc=1, device_id=device, device_id_type=MESH)

    each_local(lambda there, tx: greet({"local": there}))
    each_group(lambda there: greet({"group": there}))

    with jax.named_scope("cut_tokens"):
        for copy in small:
            copy.wait()
        meta_out[...] = jnp.zeros_like(meta_out)
        meta_out[0:tok, 0:top] = ids[...].astype(F32)
        meta_out[0:tok, top:2 * top] = gates[...].astype(F32)

        def cut(dest):
            start = pl.multiple_of(dest * w, LANES)
            for side, ref in enumerate((tokens, cotangent)):
                v = ref[:, pl.ds(start, w)].astype(F32)
                for i in range(tok):
                    for j in range(nj):
                        r = i * ns + side * nj + j
                        xs_f[dest, r:r + 1, :] = v[i:i + 1, j * LANES:(j + 1) * LANES]

        each(0, nx, cut)
        xs[...] = xs_f[...].astype(BF16)
        xr[pl.ds(at, 1)] = xs[pl.ds(x, 1)]
        meta_in[pl.ds(at, 1)] = meta_out[...].reshape(1, 8, LANES)

    with jax.named_scope("entry_wait"):
        pl.semaphore_wait(barrier, nl + ng - 2)

    def exchange(there, tx):
        remote(meta_out.at[pl.ds(0, tok)], meta_in.at[at, pl.ds(0, tok)], m_sem, (), {"local": there}).start()
        remote(xs.at[tx], xr.at[at], x_sem, (), {"local": there}).start()

    metas = all_of(meta_in.at[:, pl.ds(0, tok)], nl - 1, m_sem, ())
    blocks = all_of(xr, nl - 1, x_sem, ())

    with jax.named_scope("token_exchange"):
        each_local(exchange)
        metas.wait_recv()

    with jax.named_scope("routing"):
        xf[0:nl * 8] = meta_in[...].reshape(nl * 8, LANES)
        meta = jnp.concatenate([xf[pl.ds(i, nl, stride=8), :] for i in range(tok)], 0)
        expert = lax.broadcasted_iota(jnp.int32, (group, LANES), 1).astype(F32)
        hit = jnp.zeros((group, LANES), F32)
        weight = jnp.zeros((group, LANES), F32)
        for k in range(top):
            same = meta[:, k:k + 1] == expert
            hit = jnp.where(same, 1.0, hit)
            weight = jnp.where(same, meta[:, top + k:top + k + 1], weight)

        def order(axis):
            p = lax.broadcasted_iota(jnp.int32, (group, group), axis)
            turn = jnp.where(p >= nl, 1, 0)
            for i in range(2, tok):
                turn = jnp.where(p >= i * nl, i, turn)
            return (p - turn * nl) * tok + turn

        earlier = order(1) < order(0)
        rank = matmul(jnp.where(earlier, 1.0, 0.0).astype(BF16), hit.astype(BF16))
        kept = (hit > 0.5) & (rank < cap[...].astype(F32))
        rank = jnp.where(kept, rank, -1.0).astype(BF16)
        weight = weight.astype(BF16)

        r_group = jnp.floor((lax.broadcasted_iota(jnp.int32, (rows, LANES), 0).astype(F32) + 0.5) * (1.0 / slots))
        r_expert = r_group * ny + y.astype(F32)
        pick = jnp.where(lax.broadcasted_iota(jnp.int32, (rows, LANES), 1).astype(F32) == r_expert, 1.0, 0.0).astype(BF16)
        r_at = lax.broadcasted_iota(jnp.int32, (rows, group), 0).astype(F32)
        r_slot = r_at - jnp.floor((r_at + 0.5) * (1.0 / slots)) * slots
        select = jnp.where(matmul_t(pick, rank) == r_slot, 1.0, 0.0).astype(BF16)
        c_at = lax.broadcasted_iota(jnp.int32, (group, rows), 1).astype(F32)
        c_slot = c_at - jnp.floor((c_at + 0.5) * (1.0 / slots)) * slots
        wsel_t[...] = jnp.where(matmul_t(rank, pick) == c_slot, matmul_t(weight, pick), 0.0).astype(BF16)

    def row_blocks(way, side):
        return all_of(zr.at[way, side], ng - 1, z_sem, (way, side))

    def spread(side, way):
        def part_of(dest):
            part = rows_f[side, pl.ds(pl.multiple_of(dest * used, 8), used), :]
            if padded > used:
                part = jnp.concatenate([part, jnp.zeros((padded - used, LANES), F32)], 0)
            return part.astype(BF16)

        def go(dest):
            zs[way, side, dest] = part_of(dest)
            remote(zs.at[way, side, dest], zr.at[way, side, g], z_sem, (way, side), {"group": dest}).start()

        each_group(go)
        zr[way, side, g] = part_of(g)

    def collect(way, side):
        row_blocks(way, side).wait_recv()
        got = zr[way, side].astype(F32)
        rows_f[2 + side] = got[:, 0:used].reshape(ng * used, LANES)
        return [rows_f[2 + side, pl.ds(j, rows, stride=nj), :].astype(BF16) for j in range(nj)]

    with jax.named_scope("token_wait"):
        blocks.wait_recv()

    with jax.named_scope("row_send"):
        xf[...] = xr[...].astype(F32).reshape(nl * tok * ns, LANES)
        for side in range(2):
            for j in range(nj):
                held = jnp.concatenate(
                    [xf[pl.ds(i * ns + side * nj + j, nl, stride=tok * ns), :] for i in range(tok)], 0).astype(BF16)
                rows_f[side, pl.ds(j, rows, stride=nj), :] = matmul(select, held)
            spread(side, 0)

    def lanes_of(chunk):
        return pl.ds(pl.multiple_of(chunk * fc, LANES), fc)

    def products(kind, chunk):
        here = lanes_of(chunk)
        if kind == 0:
            both = matmul(acts[0], jnp.concatenate([wg[:, here], wu[:, here]], 1))
            return [(0, both[:, 0:fc]), (1, both[:, fc:2 * fc])]
        return [(2, matmul_t(acts[1], wd[here, :]))]

    def chunk_at(k):
        return lax.rem(x + k + nx, nx)

    FAR, THREE, ONE, TWO = range(4)
    routes = {FAR: (far_out, far_in, 2), THREE: (three_out, three_in, 1), ONE: (one_out, one_in, 1),
              TWO: (two_out, two_in, 2)}
    signs = (1, -1)

    def rs_copy(route, way, m):
        out, into, distance = routes[route]
        return remote(out.at[way, m], into.at[way, m], rs_sem, (route, way, m), x_dev(signs[way] * distance))

    def rs_far(kind):
        for m, part in products(kind, chunk_at(hx)):
            for way in range(2):
                far_out[way, m] = (part[0:half] if way == 0 else part[half:rows]).astype(BF16)
                rs_copy(FAR, way, m).start()

    def rs_plain(kind, route, distance):
        out = routes[route][0]
        for way in range(2):
            for m, part in products(kind, chunk_at(signs[way] * distance)):
                out[way, m] = part.astype(BF16)
                rs_copy(route, way, m).start()

    def rs_pass(kind):
        for way in range(2):
            for m, part in products(kind, chunk_at(signs[way] * 2)):
                rs_copy(FAR, way, m).wait_recv()
                rs_copy(THREE, way, m).wait_recv()
                part = part + three_in[way, m].astype(F32)
                add = far_in[way, m].astype(F32)
                if way == 0:
                    two_out[way, m, 0:half] = (part[0:half] + add).astype(BF16)
                    two_out[way, m, half:rows] = part[half:rows].astype(BF16)
                else:
                    two_out[way, m, 0:half] = part[0:half].astype(BF16)
                    two_out[way, m, half:rows] = (part[half:rows] + add).astype(BF16)
                rs_copy(TWO, way, m).start()

    def rs_last(kind):
        totals = []
        for m, part in products(kind, x):
            for route, ref in ((ONE, one_in), (TWO, two_in)):
                for way in range(2):
                    rs_copy(route, way, m).wait_recv()
                    part = part + ref[way, m].astype(F32)
            totals.append(part)
        return totals

    def ag_copy(way, distance, m, receive=False):
        back = distance if receive else (0 if distance <= 2 else 2)
        ref = hid.at[chunk_at(-signs[way] * back), m]
        if distance == hx:
            ref = ref.at[pl.ds(0, half)] if way == 0 else ref.at[pl.ds(half, rows - half)]
        hop = distance if distance <= 2 else distance - 2
        return remote(ref, ref, ag_sem, (way, distance - 1, m), x_dev(signs[way] * hop))

    def ag_start(m):
        for distance in (2, 1):
            for way in range(2):
                ag_copy(way, distance, m).start()

    def ag_pass(m):
        for way in range(2):
            ag_copy(way, 2, m, True).wait_recv()
            for distance in range(hx, 2, -1):
                ag_copy(way, distance, m).start()

    def ag_wait(m, distance):
        for way in range(2):
            ag_copy(way, distance, m, True).wait_recv()

    def add_out(chunk):
        acc[0] += matmul(hid[chunk, 0], wd[lanes_of(chunk), :])

    def add_grad(chunk):
        here = lanes_of(chunk)
        acc[1] += matmul_t(jnp.concatenate([hid[chunk, 1], hid[chunk, 2]], 1),
                           jnp.concatenate([wg[:, here], wu[:, here]], 1))

    def both_sides(add, distance):
        add(chunk_at(distance))
        add(chunk_at(-distance))

    with jax.named_scope("rows_wait"):
        for j, part in enumerate(collect(0, 0)):
            acts[0, :, j * LANES:(j + 1) * LANES] = part
        for copy in weights:
            copy.wait()

    with jax.named_scope("gate_up_start"):
        rs_far(0)
        rs_plain(0, THREE, 3)
        rs_plain(0, ONE, 1)

    with jax.named_scope("cotangent_wait"):
        for j, part in enumerate(collect(0, 1)):
            acts[1, :, j * LANES:(j + 1) * LANES] = part

    with jax.named_scope("back_start"):
        rs_far(1)
        rs_plain(1, THREE, 3)

    with jax.named_scope("gate_up_pass"):
        rs_pass(0)

    with jax.named_scope("back_pass"):
        rs_plain(1, ONE, 1)
        rs_pass(1)

    with jax.named_scope("gate_up_last"):
        gate_pre, up_pre = rs_last(0)
        sig = jax.nn.sigmoid(gate_pre)
        silu = gate_pre * sig
        hid[x, 0] = (silu * up_pre).astype(BF16)
        ag_start(0)
        d_gate_by = up_pre * sig * (1.0 + gate_pre * (1.0 - sig))

    with jax.named_scope("back_last"):
        acc[...] = jnp.zeros_like(acc)
        add_out(x)
        (d_hidden,) = rs_last(1)
        hid[x, 1] = (d_hidden * d_gate_by).astype(BF16)
        ag_start(1)
        hid[x, 2] = (d_hidden * silu).astype(BF16)
        ag_start(2)

    with jax.named_scope("hidden_pass"):
        add_grad(x)
        ag_pass(0)
        ag_wait(0, 1)
        both_sides(add_out, 1)
        both_sides(add_out, 2)

    with jax.named_scope("grad_pass"):
        ag_pass(1)
        ag_pass(2)

    with jax.named_scope("out_rest"):
        for distance in range(3, hx):
            ag_wait(0, distance)
            both_sides(add_out, distance)
        ag_wait(0, hx)
        add_out(chunk_at(hx))

    def send_back(side):
        for j in range(nj):
            rows_f[side, pl.ds(j, rows, stride=nj), :] = acc[side, :, j * LANES:(j + 1) * LANES]
        spread(side, 1)

    with jax.named_scope("out_send"):
        send_back(0)

    with jax.named_scope("grad_rest"):
        for m in (1, 2):
            ag_wait(m, 1)
        both_sides(add_grad, 1)
        both_sides(add_grad, 2)
        for distance in range(3, hx):
            for m in (1, 2):
                ag_wait(m, distance)
            both_sides(add_grad, distance)
        for m in (1, 2):
            ag_wait(m, hx)
        add_grad(chunk_at(hx))

    with jax.named_scope("grad_send"):
        send_back(1)

    mine = tok * ns
    sums = all_of(hi, nl - 1, h_sem, ())

    def weigh(side):
        for j, part in enumerate(collect(1, side)):
            total = matmul(wsel_t[...], part)
            for i in range(tok):
                ho_f[pl.ds((side * tok + i) * nj + j, nl, stride=mine), :] = total[i * nl:(i + 1) * nl]

    def send_home(there, tx):
        remote(ho.at[there], hi.at[at], h_sem, (), {"local": there}).start()

    with jax.named_scope("mixed_rows"):
        weigh(0)

    with jax.named_scope("grad_rows"):
        weigh(1)

    with jax.named_scope("home_send"):
        ho[...] = ho_f[...].astype(BF16).reshape(nl, mine, LANES)
        each_local(send_home)
        hi[pl.ds(at, 1)] = ho[pl.ds(at, 1)]

    with jax.named_scope("home_wait"):
        sums.wait_recv()

    with jax.named_scope("finish"):
        total = jnp.sum(hi[...].astype(F32).reshape(ny, nx, mine, LANES), axis=0)
        whole = []
        for src in range(nx):
            for j in range(nj):
                whole.append(jnp.concatenate([total[src, i * nj + j:i * nj + j + 1] for i in range(2 * tok)], 0))
        result[...] = jnp.concatenate(whole, 1)

    with jax.named_scope("drain"):
        metas.wait_send()
        blocks.wait_send()
        sums.wait_send()
        for side in range(2):
            for way in range(2):
                row_blocks(way, side).wait_send()
        for way in range(2):
            for m in range(3):
                for route in routes:
                    rs_copy(route, way, m).wait_send()
                for distance in range(1, hx + 1):
                    ag_copy(way, distance, m).wait_send()


def per_device(nx, ny, ng, tokens, cotangent, gates, expert_ids, capacity, w_gate, w_up, w_down):
    tok, width = tokens.shape
    top = expert_ids.shape[1]
    w, ff = w_gate.shape
    experts = capacity.shape[0]
    nl = nx * ny
    group = nl * tok
    slots = min(group * top // experts * 5 // 4, group)
    rows = ng * slots
    nj = w // LANES
    ns = 2 * nj
    fc = ff // nx
    padded = -(-slots * nj // 16) * 16
    cap = capacity.reshape(1, experts)
    if experts < LANES:
        cap = jnp.pad(cap, ((0, 0), (0, LANES - experts)))
    vmem = pl.BlockSpec(memory_space=pltpu.VMEM)
    hbm = pl.BlockSpec(memory_space=pl.ANY)
    dma = pltpu.SemaphoreType.DMA
    both = pl.pallas_call(
        functools.partial(moe_kernel, nx, ny, ng, slots),
        out_shape=jax.ShapeDtypeStruct((2 * tok, width), F32),
        in_specs=[hbm] * 8,
        out_specs=vmem,
        scratch_shapes=[
            pltpu.VMEM((tok, width), BF16),
            pltpu.VMEM((tok, width), BF16),
            pltpu.VMEM((tok, top), BF16),
            pltpu.VMEM((tok, top), jnp.int32),
            pltpu.VMEM(cap.shape, jnp.int32),
            pltpu.VMEM((w, ff), BF16),
            pltpu.VMEM((w, ff), BF16),
            pltpu.VMEM((ff, w), BF16),
            pltpu.VMEM((8, LANES), F32),
            pltpu.VMEM((nl, 8, LANES), F32),
            pltpu.VMEM((nx, tok * ns, LANES), F32),
            pltpu.VMEM((nx, tok * ns, LANES), BF16),
            pltpu.VMEM((nl, tok * ns, LANES), BF16),
            pltpu.VMEM((nl * tok * ns, LANES), F32),
            pltpu.VMEM((group, rows), BF16),
            pltpu.VMEM((4, rows * nj, LANES), F32),
            pltpu.VMEM((2, 2, ng, padded, LANES), BF16),
            pltpu.VMEM((2, 2, ng, padded, LANES), BF16),
            pltpu.VMEM((2, rows, w), BF16),
            pltpu.VMEM((2, 3, rows // 2, fc), BF16),
            pltpu.VMEM((2, 3, rows // 2, fc), BF16),
        ] + [pltpu.VMEM((2, 3, rows, fc), BF16)] * 6 + [
            pltpu.VMEM((nx, 3, rows, fc), BF16),
            pltpu.VMEM((2, rows, w), F32),
            pltpu.VMEM((nl * tok * ns, LANES), F32),
            pltpu.VMEM((nl, tok * ns, LANES), BF16),
            pltpu.VMEM((nl, tok * ns, LANES), BF16),
            dma((8,)),
            dma((2,)),
            dma((2,)),
            dma((2, 2, 2)),
            dma((2, 4, 2, 3)),
            dma((2, 2, nx // 2, 3)),
            dma((2,)),
        ],
        compiler_params=pltpu.CompilerParams(
            collective_id=0, has_side_effects=True, vmem_limit_bytes=60 * 1024 * 1024),
    )(tokens, cotangent, gates, expert_ids, cap, w_gate, w_up, w_down)
    return both[:tok].astype(BF16), both[tok:].astype(BF16)


def solution(mesh):
    def run(tokens, cotangent, gates, expert_ids, capacity, w_gate, w_up, w_down):
        ng, local = mesh.shape["group"], mesh.shape["local"]
        w = w_gate.shape[0] // (ng * local)
        nx = tokens.shape[1] // w
        spec = P(("group", "local"), None)
        return jax.shard_map(
            functools.partial(per_device, nx, local // nx, ng),
            mesh=mesh,
            in_specs=(spec, spec, spec, spec, P(), spec, spec, P(None, ("group", "local"))),
            out_specs=(spec, spec),
            check_vma=False,
        )(tokens, cotangent, gates, expert_ids, capacity, w_gate, w_up, w_down)

    return run
```

time: 355 us -> 92.3 us (0.26)
  waiting for transfers between devices: 225 us -> 0 us
  Pallas kernels: 0 us -> 90 us
  blocking collectives: 57.4 us -> 0 us
  starting transfers between devices: 45.8 us -> 0 us
  local copies, waits for them, and re-layouts: 11.6 us -> 0.64 us
  matrix products: 6.69 us -> 0 us
  other arithmetic: 6.21 us -> 0.85 us
    ppermute x6 -> x0, waiting for transfers between devices: 191 us -> none  [from_partner(): return lax.ppermute(block, axis, route)]
    pallas_call x0 -> x1, Pallas kernels: none -> 90 us  [per_device(): pl.pallas_call(functools.partial(moe_kernel, nx, ny, ng, slots), out_shap...]
    all_to_all x2 -> x0, blocking collectives: 57.4 us -> none  [the longest x1 33 us: cross_groups(): lax.all_to_all(values, 'group', split_axis=0, concat_axis=0, tiled=True)]
    all_to_all x4 -> x0, waiting for transfers between devices: 34.1 us -> none  [the longest x1 12.9 us: cross_groups(): lax.all_to_all(values, 'group', split_axis=0, concat_axis=0, tiled=True)]
    all_to_all x4 -> x0, starting transfers between devices: 28.7 us -> none  [the longest x1 14 us: per_device(): lax.all_to_all(send_ids, 'local', split_axis=0, concat_axis=0, tiled=True)]
    ppermute x6 -> x0, starting transfers between devices: 17.1 us -> none  [from_partner(): return lax.ppermute(block, axis, route)]
    dot_general x8 -> x0, matrix products: 6.69 us -> none  [the longest x1 1.92 us: per_device(): jnp.einsum('rf,df->rd', d_gate, w_gate, preferred_element_type=jnp.float32)]
    another operation x6 -> x0, local copies, waits for them, and re-layouts: 4.7 us -> none  [the longest x1 1.68 us: per_device(): rows_back = incoming[:, :, 1].reshape(row_total, slice_width)]
  transfers between devices with their start and end apart: 10 -> 0, of which waited for: 7 -> 0; matrix products, arithmetic and copies ran while one was open for 4% -> 0% of each run, Pallas kernels for 0% -> 0%
where the time goes in v2:
time: 92.3 us; the launch traced here: 92.1 us
  Pallas kernels  90 us (98%)
    pallas_call x1, Pallas kernels, per_device(): pl.pallas_call(functools.partial(moe_kernel, nx, ny, ng, slots), out_shap...  90 us

profile of v2, /device:TPU:1, one launch (start us, length us, event | category | flops | bytes accessed | tf_op | source)
XLA Modules:
  0.0 92.1 jit_solution(16900171356694203103)
XLA Ops:
  0.6 90.0 %shard_map.95 = f32[4,4096]{1,0:T(4,128)} custom-call(bf16[2,4096]{1,0:T(2,128)(2,1)} %tokens_hbm.1, bf16[2,4096]{1,0:T(2,128)(2,1)} %cotangent_hbm.1, bf16[2,8]{1,0:T(2,128)(2,1)} %gates_hbm.1, s32[2,8]{1,0:T(2,128)} %ids_hbm.1, s32[1,128]{1,0:T(1,128)} %bitcast.1, bf16[512,1024]{1,0:T(8,128)(2,1)} %wg_hbm.1, bf16[512,1024]{1,0:T(8,128)(2,1)} %wu_hbm.1, ...), custom_call_target="tpu_custom_call" | custom-call | tf_op jit(solution)/shard_map/pallas_call | solution.py:457
  90.6 0.9 convert.4
  91.5 0.6 fusion

commit v3 on v2

v3 whole, which is shorter than its diff:
```python
import functools

import jax
import jax.numpy as jnp
from jax import lax
from jax.experimental import pallas as pl
from jax.experimental.pallas import tpu as pltpu
from jax.sharding import PartitionSpec as P

LANES = 128
BF16 = jnp.bfloat16
F32 = jnp.float32
MESH = pl.DeviceIdType.MESH
CONTRACT_LAST = (((1,), (1,)), ((), ()))


def matmul(a, b):
    return jnp.dot(a, b, preferred_element_type=F32)


def matmul_t(a, b):
    return lax.dot_general(a, b, CONTRACT_LAST, preferred_element_type=F32)


def pieces(used):
    return -(-used // 16) * 16, used // 16 * 16


def moe_kernel(
    nx, ny, ng, slots,
    tokens_hbm, cotangent_hbm, gates_hbm, ids_hbm, cap_hbm, wg_hbm, wu_hbm, wd_hbm,
    result,
    tokens, cotangent, gates, ids, cap, wg, wu, wd,
    meta_out, meta_in, xs_f, xs, xr, xf, wsel_t, rows_f, zs, zr, acts,
    far_out, far_in, three_out, three_in, one_out, one_in, two_out, two_in, hid, acc, ho_f, ho, hi,
    load_sem, x_sem, m_sem, z_sem, rs_sem, ag_sem, sent_sem, h_sem,
):
    tok, width = tokens.shape
    top = ids.shape[1]
    w = wg.shape[0]
    fc = wg.shape[1] // nx
    nj = w // LANES
    ns = 2 * nj
    nl = nx * ny
    group = nl * tok
    rows = ng * slots
    part_rows = rows // 2
    top_rows = far_out.shape[3]
    used = slots * nj
    cuts = pieces(used)
    hx = nx // 2

    g = lax.axis_index("group")
    at = lax.axis_index("local")
    y = lax.div(at, nx)
    x = lax.rem(at, nx)

    def x_dev(k):
        return {"local": y * nx + lax.rem(x + k + nx, nx)}

    def each(low, high, body):
        def step(i, carry):
            body(i)
            return carry
        lax.fori_loop(low, high, step, 0)

    def far_first(p, n):
        return n // 2 + (p + 1) // 2 * (1 - 2 * (p % 2))

    x_order = [far_first(q, nx) for q in range(nx)]
    x_places = [lax.rem(x + k, nx) for k in x_order]

    def each_local(body):
        def line(p):
            base = lax.rem(y + ny // 2 + lax.div(p + 1, 2) * (1 - 2 * lax.rem(p, 2)), ny) * nx
            for there in x_places:
                body(base + there, there)

        each(0, ny - 1, line)
        for there in x_places[:-1]:
            body(y * nx + there, there)

    def each_group(body):
        each(0, ng - 1, lambda p: body(lax.rem(g + ng // 2 + lax.div(p + 1, 2) * (1 - 2 * lax.rem(p, 2)), ng)))

    def remote(src, dst, sems, index, device):
        return pltpu.make_async_remote_copy(
            src_ref=src, dst_ref=dst, send_sem=sems.at[(0,) + index], recv_sem=sems.at[(1,) + index],
            device_id=device, device_id_type=MESH)

    def all_of(ref, count, sems, index):
        part = ref.at[pl.ds(0, count)]
        return remote(part, part, sems, index, x_dev(1))

    loads = [pltpu.make_async_copy(a, b, load_sem.at[i]) for i, (a, b) in enumerate((
        (tokens_hbm, tokens), (cotangent_hbm, cotangent), (gates_hbm, gates), (ids_hbm, ids),
        (cap_hbm, cap), (wg_hbm, wg), (wu_hbm, wu), (wd_hbm, wd)))]
    small, weights = loads[:5], loads[5:]

    barrier = pltpu.get_barrier_semaphore()

    def greet(device):
        pl.semaphore_signal(barrier, inc=1, device_id=device, device_id_type=MESH)

    each_local(lambda there, tx: greet({"local": there}))
    each_group(lambda there: greet({"group": there}))
    for copy in loads:
        copy.start()

    with jax.named_scope("cut_tokens"):
        for copy in small:
            copy.wait()
        meta_out[...] = jnp.zeros_like(meta_out)
        meta_out[0:tok, 0:top] = ids[...].astype(F32)
        meta_out[0:tok, top:2 * top] = gates[...].astype(F32)

        def cut(dest):
            start = pl.multiple_of(dest * w, LANES)
            for side, ref in enumerate((tokens, cotangent)):
                v = ref[:, pl.ds(start, w)].astype(F32)
                for i in range(tok):
                    for j in range(nj):
                        r = i * ns + side * nj + j
                        xs_f[dest, r:r + 1, :] = v[i:i + 1, j * LANES:(j + 1) * LANES]

        each(0, nx, cut)
        xs[...] = xs_f[...].astype(BF16)
        xr[pl.ds(at, 1)] = xs[pl.ds(x, 1)]
        meta_in[pl.ds(at, 1)] = meta_out[...].reshape(1, 8, LANES)

    with jax.named_scope("entry_wait"):
        pl.semaphore_wait(barrier, nl + ng - 2)

    def exchange(there, tx):
        remote(meta_out.at[pl.ds(0, tok)], meta_in.at[at, pl.ds(0, tok)], m_sem, (), {"local": there}).start()
        remote(xs.at[tx], xr.at[at], x_sem, (), {"local": there}).start()

    metas = all_of(meta_in.at[:, pl.ds(0, tok)], nl - 1, m_sem, ())
    blocks = all_of(xr, nl - 1, x_sem, ())

    with jax.named_scope("token_exchange"):
        each_local(exchange)
        metas.wait_recv()

    with jax.named_scope("routing"):
        xf[0:nl * 8] = meta_in[...].reshape(nl * 8, LANES)
        meta = jnp.concatenate([xf[pl.ds(i, nl, stride=8), :] for i in range(tok)], 0)
        expert = lax.broadcasted_iota(jnp.int32, (group, LANES), 1).astype(F32)
        hit = jnp.zeros((group, LANES), F32)
        weight = jnp.zeros((group, LANES), F32)
        for k in range(top):
            same = meta[:, k:k + 1] == expert
            hit = jnp.where(same, 1.0, hit)
            weight = jnp.where(same, meta[:, top + k:top + k + 1], weight)

        def order(axis):
            p = lax.broadcasted_iota(jnp.int32, (group, group), axis)
            turn = jnp.where(p >= nl, 1, 0)
            for i in range(2, tok):
                turn = jnp.where(p >= i * nl, i, turn)
            return (p - turn * nl) * tok + turn

        earlier = order(1) < order(0)
        rank = matmul(jnp.where(earlier, 1.0, 0.0).astype(BF16), hit.astype(BF16))
        kept = (hit > 0.5) & (rank < cap[...].astype(F32))
        rank = jnp.where(kept, rank, -1.0).astype(BF16)
        weight = weight.astype(BF16)

        r_group = jnp.floor((lax.broadcasted_iota(jnp.int32, (rows, LANES), 0).astype(F32) + 0.5) * (1.0 / slots))
        r_expert = r_group * ny + y.astype(F32)
        pick = jnp.where(lax.broadcasted_iota(jnp.int32, (rows, LANES), 1).astype(F32) == r_expert, 1.0, 0.0).astype(BF16)
        r_at = lax.broadcasted_iota(jnp.int32, (rows, group), 0).astype(F32)
        r_slot = r_at - jnp.floor((r_at + 0.5) * (1.0 / slots)) * slots
        select = jnp.where(matmul_t(pick, rank) == r_slot, 1.0, 0.0).astype(BF16)
        c_at = lax.broadcasted_iota(jnp.int32, (group, rows), 1).astype(F32)
        c_slot = c_at - jnp.floor((c_at + 0.5) * (1.0 / slots)) * slots
        wsel_t[...] = jnp.where(matmul_t(rank, pick) == c_slot, matmul_t(weight, pick), 0.0).astype(BF16)

    def piece(way, index):
        low, high = (0, cuts[way]) if index == 0 else (cuts[way], 2 * used)
        return pl.ds(low, high - low)

    def row_blocks(way, index):
        return all_of(zr.at[way, :, piece(way, index)], ng - 1, z_sem, (way, index))

    def spread(way, index):
        low, high = (0, cuts[way]) if index == 0 else (cuts[way], 2 * used)
        here = piece(way, index)

        def part_of(dest):
            start = pl.multiple_of(dest * used, 8)
            parts = []
            if low < used:
                parts.append(rows_f[0, pl.ds(start + low, min(high, used) - low), :])
            if high > used:
                first = max(low, used)
                parts.append(rows_f[1, pl.ds(start + first - used, high - first), :])
            return jnp.concatenate(parts, 0).astype(BF16)

        def go(dest):
            zs[way, dest, here] = part_of(dest)
            remote(zs.at[way, dest, here], zr.at[way, g, here], z_sem, (way, index), {"group": dest}).start()

        each_group(go)
        zr[way, g, here] = part_of(g)

    def lay_out(side, got):
        rows_f[2 + side] = got.astype(F32).reshape(ng * used, LANES)
        return [rows_f[2 + side, pl.ds(j, rows, stride=nj), :].astype(BF16) for j in range(nj)]

    with jax.named_scope("token_wait"):
        blocks.wait_recv()

    with jax.named_scope("row_send"):
        xf[...] = xr[...].astype(F32).reshape(nl * tok * ns, LANES)
        for side in range(2):
            for j in range(nj):
                held = jnp.concatenate(
                    [xf[pl.ds(i * ns + side * nj + j, nl, stride=tok * ns), :] for i in range(tok)], 0).astype(BF16)
                rows_f[side, pl.ds(j, rows, stride=nj), :] = matmul(select, held)
        spread(0, 0)
        spread(0, 1)

    def lanes_of(chunk):
        return pl.ds(pl.multiple_of(chunk * fc, LANES), fc)

    def of(part):
        return pl.ds(part * part_rows, part_rows)

    def products(kind, part, chunk):
        here = lanes_of(chunk)
        if kind == 0:
            both = matmul(acts[0, of(part)], jnp.concatenate([wg[:, here], wu[:, here]], 1))
            return [(0, both[:, 0:fc]), (1, both[:, fc:2 * fc])]
        return [(2, matmul_t(acts[1, of(part)], wd[here, :]))]

    def chunk_at(k):
        return lax.rem(x + k + nx, nx)

    FAR, THREE, TWO, ONE = range(4)
    routes = {FAR: (far_out, far_in, 2), THREE: (three_out, three_in, 1), TWO: (two_out, two_in, 1),
              ONE: (one_out, one_in, 1)}
    signs = (1, -1)
    rs_kinds = (pl.ds(0, 2), pl.ds(2, 1))
    ag_kinds = (pl.ds(0, 1), pl.ds(1, 2))

    def far_span(part, way):
        cut = top_rows if part == 0 else part_rows - top_rows
        return (0, cut) if way == 0 else (cut, part_rows)

    def one_way(src, dst, send_sem, recv_sem, device):
        return pltpu.make_async_remote_copy(
            src_ref=src, dst_ref=dst, send_sem=send_sem, recv_sem=recv_sem, device_id=device, device_id_type=MESH)

    def rs_copy(route, way, kind, part):
        out, into, distance = routes[route]
        out, into = out.at[part, way, rs_kinds[kind]], into.at[part, way, rs_kinds[kind]]
        if route == FAR:
            low, high = far_span(part, way)
            out, into = out.at[:, pl.ds(0, high - low)], into.at[:, pl.ds(0, high - low)]
        return one_way(out, into, sent_sem.at[0, part], rs_sem.at[route, way, kind, part], x_dev(signs[way] * distance))

    def rs_start(kind, part):
        shared = products(kind, part, chunk_at(hx))
        for way in range(2):
            low, high = far_span(part, way)
            for m, value in shared:
                far_out[part, way, m, 0:high - low] = value[low:high].astype(BF16)
            rs_copy(FAR, way, kind, part).start()
        for way in range(2):
            for m, value in products(kind, part, chunk_at(signs[way] * 3)):
                three_out[part, way, m] = value.astype(BF16)
            rs_copy(THREE, way, kind, part).start()

    def rs_two(kind, part):
        for way in range(2):
            mine = products(kind, part, chunk_at(signs[way] * 2))
            rs_copy(FAR, way, kind, part).wait_recv()
            rs_copy(THREE, way, kind, part).wait_recv()
            low, high = far_span(part, way)
            for m, value in mine:
                value = value + three_in[part, way, m].astype(F32)
                add = value[low:high] + far_in[part, way, m, 0:high - low].astype(F32)
                two_out[part, way, m, low:high] = add.astype(BF16)
                if way == 0:
                    two_out[part, way, m, high:part_rows] = value[high:part_rows].astype(BF16)
                else:
                    two_out[part, way, m, 0:low] = value[0:low].astype(BF16)
            rs_copy(TWO, way, kind, part).start()

    def rs_one(kind, part):
        for way in range(2):
            mine = products(kind, part, chunk_at(signs[way]))
            rs_copy(TWO, way, kind, part).wait_recv()
            for m, value in mine:
                one_out[part, way, m] = (value + two_in[part, way, m].astype(F32)).astype(BF16)
            rs_copy(ONE, way, kind, part).start()

    def rs_last(kind, part):
        mine = products(kind, part, x)
        for way in range(2):
            rs_copy(ONE, way, kind, part).wait_recv()
        return [value + (one_in[part, 0, m].astype(F32) + one_in[part, 1, m].astype(F32)) for m, value in mine]

    def ag_copy(way, distance, kind, part, receive=False):
        back = distance if receive else min(distance - 1, 2)
        ref = hid.at[part, chunk_at(-signs[way] * back), ag_kinds[kind]]
        if distance == hx:
            low, high = far_span(part, way)
            ref = ref.at[:, pl.ds(low, high - low)]
        hop = distance - min(distance - 1, 2)
        return one_way(ref, ref, sent_sem.at[1, part], ag_sem.at[way, distance - 1, kind, part], x_dev(signs[way] * hop))

    def ag_start(kind, part):
        for way in range(2):
            ag_copy(way, 1, kind, part).start()

    def ag_pass(kind, part, distance):
        for way in range(2):
            ag_copy(way, distance, kind, part, True).wait_recv()
            for further in (2,) if distance == 1 else range(hx, 2, -1):
                ag_copy(way, further, kind, part).start()

    def ag_wait(kind, part, distance):
        for way in range(2):
            ag_copy(way, distance, kind, part, True).wait_recv()

    def add_out(part, k):
        chunk = chunk_at(k)
        acc[0, of(part)] += matmul(hid[part, chunk, 0], wd[lanes_of(chunk), :])

    def add_grad(part, k):
        chunk = chunk_at(k)
        here = lanes_of(chunk)
        acc[1, of(part)] += matmul_t(jnp.concatenate([hid[part, chunk, 1], hid[part, chunk, 2]], 1),
                                     jnp.concatenate([wg[:, here], wu[:, here]], 1))

    adds = (add_out, add_grad)

    def add_both(kind, part, distance):
        adds[kind](part, distance)
        adds[kind](part, -distance)

    def add_rest(kind):
        for distance in range(3, hx):
            for part in range(2):
                ag_wait(kind, part, distance)
                add_both(kind, part, distance)
        for part in range(2):
            ag_wait(kind, part, hx)
            adds[kind](part, hx)

    with jax.named_scope("rows_wait"):
        row_blocks(0, 0).wait_recv()
        for j, part in enumerate(lay_out(0, zr[0, :, 0:cuts[0]].astype(F32)[:, 0:used])):
            acts[0, :, j * LANES:(j + 1) * LANES] = part
        for copy in weights:
            copy.wait()

    with jax.named_scope("gate_up_start"):
        for part in range(2):
            rs_start(0, part)

    with jax.named_scope("cotangent_wait"):
        row_blocks(0, 1).wait_recv()
        for j, part in enumerate(lay_out(1, zr[0].astype(F32)[:, used:2 * used])):
            acts[1, :, j * LANES:(j + 1) * LANES] = part

    with jax.named_scope("back_start"):
        for part in range(2):
            rs_start(1, part)

    with jax.named_scope("gate_up_two"):
        for part in range(2):
            rs_two(0, part)

    with jax.named_scope("back_two"):
        for part in range(2):
            rs_two(1, part)

    with jax.named_scope("gate_up_one"):
        for part in range(2):
            rs_one(0, part)

    with jax.named_scope("back_one"):
        acc[...] = jnp.zeros_like(acc)
        for part in range(2):
            rs_one(1, part)

    with jax.named_scope("gate_up_last"):
        saved = []
        for part in range(2):
            gate_pre, up_pre = rs_last(0, part)
            sig = jax.nn.sigmoid(gate_pre)
            silu = gate_pre * sig
            hid[part, x, 0] = (silu * up_pre).astype(BF16)
            ag_start(0, part)
            saved.append((up_pre * sig * (1.0 + gate_pre * (1.0 - sig)), silu))

    with jax.named_scope("back_last"):
        for part in range(2):
            (d_hidden,) = rs_last(1, part)
            hid[part, x, 1] = (d_hidden * saved[part][0]).astype(BF16)
            hid[part, x, 2] = (d_hidden * saved[part][1]).astype(BF16)
            ag_start(1, part)

    with jax.named_scope("hidden_pass_one"):
        for part in range(2):
            add_out(part, 0)
            ag_pass(0, part, 1)

    with jax.named_scope("grad_pass_one"):
        for part in range(2):
            add_grad(part, 0)
            ag_pass(1, part, 1)

    with jax.named_scope("hidden_pass_two"):
        for part in range(2):
            add_both(0, part, 1)
            ag_pass(0, part, 2)

    with jax.named_scope("grad_pass_two"):
        for part in range(2):
            add_both(1, part, 1)
            ag_pass(1, part, 2)

    with jax.named_scope("out_rest"):
        for part in range(2):
            add_both(0, part, 2)
        add_rest(0)

    def send_back(side):
        for j in range(nj):
            rows_f[side, pl.ds(j, rows, stride=nj), :] = acc[side, :, j * LANES:(j + 1) * LANES]
        spread(1, side)

    with jax.named_scope("out_send"):
        send_back(0)

    with jax.named_scope("grad_rest"):
        for part in range(2):
            add_both(1, part, 2)
        add_rest(1)

    with jax.named_scope("grad_send"):
        send_back(1)

    mine = tok * ns
    sums = all_of(hi, nl - 1, h_sem, ())

    def weigh(side):
        for j, part in enumerate(lay_out(side, zr[1].astype(F32)[:, side * used:(side + 1) * used])):
            total = matmul(wsel_t[...], part)
            for i in range(tok):
                ho_f[pl.ds((side * tok + i) * nj + j, nl, stride=mine), :] = total[i * nl:(i + 1) * nl]

    def send_home(there, tx):
        remote(ho.at[there], hi.at[at], h_sem, (), {"local": there}).start()

    with jax.named_scope("back_wait"):
        for index in range(2):
            row_blocks(1, index).wait_recv()

    with jax.named_scope("grad_rows"):
        for side in range(2):
            weigh(side)

    with jax.named_scope("home_send"):
        ho[...] = ho_f[...].astype(BF16).reshape(nl, mine, LANES)
        each_local(send_home)
        hi[pl.ds(at, 1)] = ho[pl.ds(at, 1)]

    with jax.named_scope("home_wait"):
        sums.wait_recv()

    with jax.named_scope("finish"):
        total = jnp.sum(hi[...].astype(F32).reshape(ny, nx, mine, LANES), axis=0)
        whole = []
        for src in range(nx):
            for j in range(nj):
                whole.append(jnp.concatenate([total[src, i * nj + j:i * nj + j + 1] for i in range(2 * tok)], 0))
        result[...] = jnp.concatenate(whole, 1).astype(BF16)

    with jax.named_scope("drain"):
        metas.wait_send()
        blocks.wait_send()
        sums.wait_send()
        for index in range(2):
            for way in range(2):
                row_blocks(way, index).wait_send()
        for stage in range(2):
            for part in range(2):
                chunks = hid.at[part, pl.ds(0, nx - 1)]
                one_way(chunks, chunks, sent_sem.at[stage, part], rs_sem.at[0, 0, 0, 0], x_dev(1)).wait_send()


def per_device(nx, ny, ng, tokens, cotangent, gates, expert_ids, capacity, w_gate, w_up, w_down):
    tok, width = tokens.shape
    top = expert_ids.shape[1]
    w, ff = w_gate.shape
    experts = capacity.shape[0]
    nl = nx * ny
    group = nl * tok
    slots = min(group * top // experts * 5 // 4, group)
    rows = ng * slots
    nj = w // LANES
    ns = 2 * nj
    fc = ff // nx
    part_rows = rows // 2
    top_rows = -(-part_rows // 32) * 16
    if top_rows >= part_rows:
        top_rows = part_rows // 2
    cap = capacity.reshape(1, experts)
    if experts < LANES:
        cap = jnp.pad(cap, ((0, 0), (0, LANES - experts)))
    vmem = pl.BlockSpec(memory_space=pltpu.VMEM)
    hbm = pl.BlockSpec(memory_space=pl.ANY)
    dma = pltpu.SemaphoreType.DMA
    both = pl.pallas_call(
        functools.partial(moe_kernel, nx, ny, ng, slots),
        out_shape=pltpu.VMEM((2 * tok, width), BF16),
        in_specs=[hbm] * 8,
        out_specs=vmem,
        scratch_shapes=[
            pltpu.VMEM((tok, width), BF16),
            pltpu.VMEM((tok, width), BF16),
            pltpu.VMEM((tok, top), BF16),
            pltpu.VMEM((tok, top), jnp.int32),
            pltpu.VMEM(cap.shape, jnp.int32),
            pltpu.VMEM((w, ff), BF16),
            pltpu.VMEM((w, ff), BF16),
            pltpu.VMEM((ff, w), BF16),
            pltpu.VMEM((8, LANES), F32),
            pltpu.VMEM((nl, 8, LANES), F32),
            pltpu.VMEM((nx, tok * ns, LANES), F32),
            pltpu.VMEM((nx, tok * ns, LANES), BF16),
            pltpu.VMEM((nl, tok * ns, LANES), BF16),
            pltpu.VMEM((nl * tok * ns, LANES), F32),
            pltpu.VMEM((group, rows), BF16),
            pltpu.VMEM((4, rows * nj, LANES), F32),
            pltpu.VMEM((2, ng, 2 * slots * nj, LANES), BF16),
            pltpu.VMEM((2, ng, 2 * slots * nj, LANES), BF16),
            pltpu.VMEM((2, rows, w), BF16),
            pltpu.VMEM((2, 2, 3, top_rows, fc), BF16),
            pltpu.VMEM((2, 2, 3, top_rows, fc), BF16),
        ] + [pltpu.VMEM((2, 2, 3, part_rows, fc), BF16)] * 6 + [
            pltpu.VMEM((2, nx, 3, part_rows, fc), BF16),
            pltpu.VMEM((2, rows, w), F32),
            pltpu.VMEM((nl * tok * ns, LANES), F32),
            pltpu.VMEM((nl, tok * ns, LANES), BF16),
            pltpu.VMEM((nl, tok * ns, LANES), BF16),
            dma((8,)),
            dma((2,)),
            dma((2,)),
            dma((2, 2, 2)),
            dma((4, 2, 2, 2)),
            dma((2, nx // 2, 2, 2)),
            dma((2, 2)),
            dma((2,)),
        ],
        compiler_params=pltpu.CompilerParams(
            collective_id=0, has_side_effects=True, vmem_limit_bytes=60 * 1024 * 1024),
    )(tokens, cotangent, gates, expert_ids, cap, w_gate, w_up, w_down)
    return both[:tok], both[tok:]


def solution(mesh):
    def run(tokens, cotangent, gates, expert_ids, capacity, w_gate, w_up, w_down):
        ng, local = mesh.shape["group"], mesh.shape["local"]
        w = w_gate.shape[0] // (ng * local)
        nx = tokens.shape[1] // w
        spec = P(("group", "local"), None)
        return jax.shard_map(
            functools.partial(per_device, nx, local // nx, ng),
            mesh=mesh,
            in_specs=(spec, spec, spec, spec, P(), spec, spec, P(None, ("group", "local"))),
            out_specs=(spec, spec),
            check_vma=False,
        )(tokens, cotangent, gates, expert_ids, capacity, w_gate, w_up, w_down)

    return run
```

time: 92.3 us -> 87.5 us (0.948)
  Pallas kernels: 90 us -> 86.1 us
    pallas_call x1, Pallas kernels: 90 us -> 86.1 us  [per_device(): pl.pallas_call(functools.partial(moe_kernel, nx, ny, ng, slots), out_shap...]
where the time goes in v3:
time: 87.5 us; the launch traced here: 87.3 us
  Pallas kernels  86.1 us (98%)
    pallas_call x1, Pallas kernels, per_device(): pl.pallas_call(functools.partial(moe_kernel, nx, ny, ng, slots), out_shap...  86.1 us

profile of v3, /device:TPU:1, one launch (start us, length us, event | category | flops | bytes accessed | tf_op | source)
XLA Modules:
  0.0 87.3 jit_solution(2059644366160388342)
XLA Ops:
  0.6 86.1 %shard_map.95 = bf16[4,4096]{1,0:T(4,128)(2,1)S(1)} custom-call(bf16[2,4096]{1,0:T(2,128)(2,1)} %tokens_hbm.1, bf16[2,4096]{1,0:T(2,128)(2,1)} %cotangent_hbm.1, bf16[2,8]{1,0:T(2,128)(2,1)} %gates_hbm.1, s32[2,8]{1,0:T(2,128)} %ids_hbm.1, s32[1,128]{1,0:T(1,128)} %bitcast.1, bf16[512,1024]{1,0:T(8,128)(2,1)} %wg_hbm.1, bf16[512,1024]{1,0:T(8,128)(2,1)} %wu_hbm.1, ...), custom_call_target="tpu_custom_call" | custom-call | tf_op jit(solution)/shard_map/pallas_call | solution.py:519
  86.7 0.6 fusion

commit v4 on v3

--- a/solution.py
+++ b/solution.py
@@ -32,7 +32,7 @@
     result,
     tokens, cotangent, gates, ids, cap, wg, wu, wd,
     meta_out, meta_in, xs_f, xs, xr, xf, wsel_t, rows_f, zs, zr, acts,
-    far_out, far_in, three_out, three_in, one_out, one_in, two_out, two_in, hid, acc, ho_f, ho, hi,
+    far_out, far_in, three_out, three_in, one_out, one_in, two_out, two_in, made, hid, acc, ho_f, ho, hi,
     load_sem, x_sem, m_sem, z_sem, rs_sem, ag_sem, sent_sem, h_sem,
 ):
     tok, width = tokens.shape
@@ -70,13 +70,17 @@
     x_order = [far_first(q, nx) for q in range(nx)]
     x_places = [lax.rem(x + k, nx) for k in x_order]
 
-    def each_local(body):
+    def each_local(body, ahead=None):
         def line(p):
-            base = lax.rem(y + ny // 2 + lax.div(p + 1, 2) * (1 - 2 * lax.rem(p, 2)), ny) * nx
+            there_y = lax.rem(y + ny // 2 + lax.div(p + 1, 2) * (1 - 2 * lax.rem(p, 2)), ny)
+            if ahead is not None:
+                ahead(there_y)
             for there in x_places:
-                body(base + there, there)
+                body(there_y * nx + there, there)
 
         each(0, ny - 1, line)
+        if ahead is not None:
+            ahead(y)
         for there in x_places[:-1]:
             body(y * nx + there, there)
 
@@ -131,15 +135,18 @@
     with jax.named_scope("entry_wait"):
         pl.semaphore_wait(barrier, nl + ng - 2)
 
-    def exchange(there, tx):
+    def send_meta(there, tx):
         remote(meta_out.at[pl.ds(0, tok)], meta_in.at[at, pl.ds(0, tok)], m_sem, (), {"local": there}).start()
+
+    def send_block(there, tx):
         remote(xs.at[tx], xr.at[at], x_sem, (), {"local": there}).start()
 
     metas = all_of(meta_in.at[:, pl.ds(0, tok)], nl - 1, m_sem, ())
     blocks = all_of(xr, nl - 1, x_sem, ())
 
     with jax.named_scope("token_exchange"):
-        each_local(exchange)
+        each_local(send_meta)
+        each_local(send_block)
         metas.wait_recv()
 
     with jax.named_scope("routing"):
@@ -227,15 +234,25 @@
     def of(part):
         return pl.ds(part * part_rows, part_rows)
 
-    def products(kind, part, chunk):
-        here = lanes_of(chunk)
-        if kind == 0:
-            both = matmul(acts[0, of(part)], jnp.concatenate([wg[:, here], wu[:, here]], 1))
-            return [(0, both[:, 0:fc]), (1, both[:, fc:2 * fc])]
-        return [(2, matmul_t(acts[1, of(part)], wd[here, :]))]
-
     def chunk_at(k):
         return lax.rem(x + k + nx, nx)
+
+    def products(kind, k):
+        here = lanes_of(chunk_at(k))
+        if kind == 0:
+            both = matmul(acts[0], jnp.concatenate([wg[:, here], wu[:, here]], 1))
+            return [(0, both[:, 0:fc]), (1, both[:, fc:2 * fc])]
+        return [(2, matmul_t(acts[1], wd[here, :]))]
+
+    near = (2, -2, 1, -1, 0)
+
+    def products_ahead(kind):
+        for index, k in enumerate(near):
+            for m, value in products(kind, k):
+                made[index, m] = value
+
+    def ready(kind, part, k):
+        return [(m, made[near.index(k), m, of(part)]) for m in ((0, 1), (2,))[kind]]
 
     FAR, THREE, TWO, ONE = range(4)
     routes = {FAR: (far_out, far_in, 2), THREE: (three_out, three_in, 1), TWO: (two_out, two_in, 1),
@@ -260,21 +277,27 @@
             out, into = out.at[:, pl.ds(0, high - low)], into.at[:, pl.ds(0, high - low)]
         return one_way(out, into, sent_sem.at[0, part], rs_sem.at[route, way, kind, part], x_dev(signs[way] * distance))
 
-    def rs_start(kind, part):
-        shared = products(kind, part, chunk_at(hx))
+    def rs_start(kind):
+        shared = products(kind, hx)
+        for part in range(2):
+            first = part * part_rows
+            for way in range(2):
+                low, high = far_span(part, way)
+                for m, value in shared:
+                    far_out[part, way, m, 0:high - low] = value[first + low:first + high].astype(BF16)
+                rs_copy(FAR, way, kind, part).start()
+        threes = []
         for way in range(2):
-            low, high = far_span(part, way)
-            for m, value in shared:
-                far_out[part, way, m, 0:high - low] = value[low:high].astype(BF16)
-            rs_copy(FAR, way, kind, part).start()
-        for way in range(2):
-            for m, value in products(kind, part, chunk_at(signs[way] * 3)):
-                three_out[part, way, m] = value.astype(BF16)
-            rs_copy(THREE, way, kind, part).start()
+            threes.append(products(kind, signs[way] * 3))
+        for part in range(2):
+            for way in range(2):
+                for m, value in threes[way]:
+                    three_out[part, way, m] = value[part * part_rows:(part + 1) * part_rows].astype(BF16)
+                rs_copy(THREE, way, kind, part).start()
 
     def rs_two(kind, part):
         for way in range(2):
-            mine = products(kind, part, chunk_at(signs[way] * 2))
+            mine = ready(kind, part, signs[way] * 2)
             rs_copy(FAR, way, kind, part).wait_recv()
             rs_copy(THREE, way, kind, part).wait_recv()
             low, high = far_span(part, way)
@@ -290,14 +313,14 @@
 
     def rs_one(kind, part):
         for way in range(2):
-            mine = products(kind, part, chunk_at(signs[way]))
+            mine = ready(kind, part, signs[way])
             rs_copy(TWO, way, kind, part).wait_recv()
             for m, value in mine:
                 one_out[part, way, m] = (value + two_in[part, way, m].astype(F32)).astype(BF16)
             rs_copy(ONE, way, kind, part).start()
 
     def rs_last(kind, part):
-        mine = products(kind, part, x)
+        mine = ready(kind, part, 0)
         for way in range(2):
             rs_copy(ONE, way, kind, part).wait_recv()
         return [value + (one_in[part, 0, m].astype(F32) + one_in[part, 1, m].astype(F32)) for m, value in mine]
@@ -358,8 +381,7 @@
             copy.wait()
 
     with jax.named_scope("gate_up_start"):
-        for part in range(2):
-            rs_start(0, part)
+        rs_start(0)
 
     with jax.named_scope("cotangent_wait"):
         row_blocks(0, 1).wait_recv()
@@ -367,12 +389,16 @@
             acts[1, :, j * LANES:(j + 1) * LANES] = part
 
     with jax.named_scope("back_start"):
-        for part in range(2):
-            rs_start(1, part)
+        rs_start(1)
+
+    with jax.named_scope("products_ahead"):
+        products_ahead(0)
 
     with jax.named_scope("gate_up_two"):
-        for part in range(2):
-            rs_two(0, part)
+        rs_two(0, 0)
+        products_ahead(1)
+        acc[...] = jnp.zeros_like(acc)
+        rs_two(0, 1)
 
     with jax.named_scope("back_two"):
         for part in range(2):
@@ -383,7 +409,6 @@
             rs_one(0, part)
 
     with jax.named_scope("back_one"):
-        acc[...] = jnp.zeros_like(acc)
         for part in range(2):
             rs_one(1, part)
 
@@ -457,6 +482,11 @@
     def send_home(there, tx):
         remote(ho.at[there], hi.at[at], h_sem, (), {"local": there}).start()
 
+    def round_line(line):
+        size = nx * mine
+        start = pl.multiple_of(line * size, size)
+        ho[pl.ds(line * nx, nx)] = ho_f[pl.ds(start, size), :].astype(BF16).reshape(nx, mine, LANES)
+
     with jax.named_scope("back_wait"):
         for index in range(2):
             row_blocks(1, index).wait_recv()
@@ -466,8 +496,7 @@
             weigh(side)
 
     with jax.named_scope("home_send"):
-        ho[...] = ho_f[...].astype(BF16).reshape(nl, mine, LANES)
-        each_local(send_home)
+        each_local(send_home, round_line)
         hi[pl.ds(at, 1)] = ho[pl.ds(at, 1)]
 
     with jax.named_scope("home_wait"):
@@ -544,6 +573,7 @@
             pltpu.VMEM((2, 2, 3, top_rows, fc), BF16),
             pltpu.VMEM((2, 2, 3, top_rows, fc), BF16),
         ] + [pltpu.VMEM((2, 2, 3, part_rows, fc), BF16)] * 6 + [
+            pltpu.VMEM((5, 3, rows, fc), F32),
             pltpu.VMEM((2, nx, 3, part_rows, fc), BF16),
             pltpu.VMEM((2, rows, w), F32),
             pltpu.VMEM((nl * tok * ns, LANES), F32),

time: 87.5 us -> 86.5 us (0.989)
  Pallas kernels: 86.1 us -> 85.1 us
    pallas_call x1, Pallas kernels: 86.1 us -> 85.1 us  [per_device(): pl.pallas_call(functools.partial(moe_kernel, nx, ny, ng, slots), out_shap...]
where the time goes in v4:
time: 86.5 us; the launch traced here: 86.3 us
  Pallas kernels  85.1 us (98%)
    pallas_call x1, Pallas kernels, per_device(): pl.pallas_call(functools.partial(moe_kernel, nx, ny, ng, slots), out_shap...  85.1 us

profile of v4, /device:TPU:1, one launch (start us, length us, event | category | flops | bytes accessed | tf_op | source)
XLA Modules:
  0.0 86.3 jit_solution(53907492186024269)
XLA Ops:
  0.6 85.1 %shard_map.95 = bf16[4,4096]{1,0:T(4,128)(2,1)S(1)} custom-call(bf16[2,4096]{1,0:T(2,128)(2,1)} %tokens_hbm.1, bf16[2,4096]{1,0:T(2,128)(2,1)} %cotangent_hbm.1, bf16[2,8]{1,0:T(2,128)(2,1)} %gates_hbm.1, s32[2,8]{1,0:T(2,128)} %ids_hbm.1, s32[1,128]{1,0:T(1,128)} %bitcast.1, bf16[512,1024]{1,0:T(8,128)(2,1)} %wg_hbm.1, bf16[512,1024]{1,0:T(8,128)(2,1)} %wu_hbm.1, ...), custom_call_target="tpu_custom_call" | custom-call | tf_op jit(solution)/shard_map/pallas_call | solution.py:548
  85.7 0.6 fusion

commit v5 on v4

--- a/solution.py
+++ b/solution.py
@@ -237,18 +237,18 @@
     def chunk_at(k):
         return lax.rem(x + k + nx, nx)
 
-    def products(kind, k):
+    def products(kind, here_rows, k):
         here = lanes_of(chunk_at(k))
         if kind == 0:
-            both = matmul(acts[0], jnp.concatenate([wg[:, here], wu[:, here]], 1))
+            both = matmul(acts[0, here_rows], jnp.concatenate([wg[:, here], wu[:, here]], 1))
             return [(0, both[:, 0:fc]), (1, both[:, fc:2 * fc])]
-        return [(2, matmul_t(acts[1], wd[here, :]))]
+        return [(2, matmul_t(acts[1, here_rows], wd[here, :]))]
 
     near = (2, -2, 1, -1, 0)
 
     def products_ahead(kind):
         for index, k in enumerate(near):
-            for m, value in products(kind, k):
+            for m, value in products(kind, pl.ds(0, rows), k):
                 made[index, m] = value
 
     def ready(kind, part, k):
@@ -277,23 +277,17 @@
             out, into = out.at[:, pl.ds(0, high - low)], into.at[:, pl.ds(0, high - low)]
         return one_way(out, into, sent_sem.at[0, part], rs_sem.at[route, way, kind, part], x_dev(signs[way] * distance))
 
-    def rs_start(kind):
-        shared = products(kind, hx)
-        for part in range(2):
-            first = part * part_rows
-            for way in range(2):
-                low, high = far_span(part, way)
-                for m, value in shared:
-                    far_out[part, way, m, 0:high - low] = value[first + low:first + high].astype(BF16)
-                rs_copy(FAR, way, kind, part).start()
-        threes = []
-        for way in range(2):
-            threes.append(products(kind, signs[way] * 3))
-        for part in range(2):
-            for way in range(2):
-                for m, value in threes[way]:
-                    three_out[part, way, m] = value[part * part_rows:(part + 1) * part_rows].astype(BF16)
-                rs_copy(THREE, way, kind, part).start()
+    def rs_start(kind, part):
+        shared = products(kind, of(part), hx)
+        for way in range(2):
+            low, high = far_span(part, way)
+            for m, value in shared:
+                far_out[part, way, m, 0:high - low] = value[low:high].astype(BF16)
+            rs_copy(FAR, way, kind, part).start()
+        for way in range(2):
+            for m, value in products(kind, of(part), signs[way] * 3):
+                three_out[part, way, m] = value.astype(BF16)
+            rs_copy(THREE, way, kind, part).start()
 
     def rs_two(kind, part):
         for way in range(2):
@@ -381,7 +375,8 @@
             copy.wait()
 
     with jax.named_scope("gate_up_start"):
-        rs_start(0)
+        for part in range(2):
+            rs_start(0, part)
 
     with jax.named_scope("cotangent_wait"):
         row_blocks(0, 1).wait_recv()
@@ -389,7 +384,8 @@
             acts[1, :, j * LANES:(j + 1) * LANES] = part
 
     with jax.named_scope("back_start"):
-        rs_start(1)
+        for part in range(2):
+            rs_start(1, part)
 
     with jax.named_scope("products_ahead"):
         products_ahead(0)

time: 86.5 us -> 86.5 us (level)
  no operation moved by 1% of the time
where the time goes in v5:
time: 86.5 us; the launch traced here: 86.3 us
  Pallas kernels  85 us (98%)
    pallas_call x1, Pallas kernels, per_device(): pl.pallas_call(functools.partial(moe_kernel, nx, ny, ng, slots), out_shap...  85 us

profile of v5, /device:TPU:1, one launch (start us, length us, event | category | flops | bytes accessed | tf_op | source)
XLA Modules:
  0.0 86.3 jit_solution(2729402473226211902)
XLA Ops:
  0.6 85.0 %shard_map.95 = bf16[4,4096]{1,0:T(4,128)(2,1)S(1)} custom-call(bf16[2,4096]{1,0:T(2,128)(2,1)} %tokens_hbm.1, bf16[2,4096]{1,0:T(2,128)(2,1)} %cotangent_hbm.1, bf16[2,8]{1,0:T(2,128)(2,1)} %gates_hbm.1, s32[2,8]{1,0:T(2,128)} %ids_hbm.1, s32[1,128]{1,0:T(1,128)} %bitcast.1, bf16[512,1024]{1,0:T(8,128)(2,1)} %wg_hbm.1, bf16[512,1024]{1,0:T(8,128)(2,1)} %wu_hbm.1, ...), custom_call_target="tpu_custom_call" | custom-call | tf_op jit(solution)/shard_map/pallas_call | solution.py:544
  85.6 0.6 fusion
